TPU v7x, 32 devices: a whole 2x2x4 slice. The times are simulated.
32 devices in a mesh: gx: 2 (over x), gy: 4 (over y, core), gz: 4 (over z).
Axes of the slice: x: 2, y: 2, z: 4, core: 2. Of those that a mesh axis runs over, the one named last changes fastest.
Arguments:
- state_real: float32 [4194304], P(('gx', 'gy', 'gz'))
- state_imag: float32 [4194304], P(('gx', 'gy', 'gz'))
- adjoint_real: float32 [4194304], P(('gx', 'gy', 'gz'))
- adjoint_imag: float32 [4194304], P(('gx', 'gy', 'gz'))
- energies: int32 [4194304], P(('gx', 'gy', 'gz')), may hold values from 11 to 3311, as said below
- gamma_angle: float32 [1], replicated, may hold values from 0.02 to 0.1
- beta_angle: float32 [1], replicated, may hold values from 0.1 to 0.7
Outputs:
- input_real: float32 [4194304], P(('gx', 'gy', 'gz'))
- input_imag: float32 [4194304], P(('gx', 'gy', 'gz'))
- adjoint_in_real: float32 [4194304], P(('gx', 'gy', 'gz'))
- adjoint_in_imag: float32 [4194304], P(('gx', 'gy', 'gz'))
- gamma_gradient: float32 [1], replicated
- beta_gradient: float32 [1], replicated
Inputs may be any that keep to these rules, and one draw needn't show every extreme that they name: `energies`: entry j is the LABS energy sum over k from 1 to 21 of (sum over i of s_i s_(i+k))^2, with spins s_i = 1 - 2 b_i from the bits b of j XOR a mask of 22 bits drawn once.
All inputs are finite; a program needn't handle non-finite values.
Results may differ from a plain program's by a relative error of at most 0.00013.
Values sent between devices are 32-bit elements; how exact they have to be, the bound alone decides.
No kernel may reach another device: no remote copies, remote signals or barrier semaphores. Data moves between devices by JAX's collectives and lax.ppermute only.
A program may use at most 64 MiB of HBM per device.

v0:
```python
import jax
import jax.numpy as jnp
from jax import lax
from jax.sharding import PartitionSpec as P


def count_ones(values, width):
    total = jnp.zeros_like(values)
    for bit_pos in range(width):
        total = total + (values >> bit_pos & 1)
    return total


def hadamard(group_bits):
    indices = jnp.arange(2**group_bits, dtype=jnp.int32)
    parity = count_ones(indices[:, None] & indices[None, :], group_bits) & 1
    return (1 - 2 * parity).astype(jnp.float32) * jnp.float32(2.0 ** (-0.5 * group_bits))


def walsh_local(values, total_bits):
    finished = 0
    while finished < total_bits:
        group_bits = min(7, total_bits - finished)
        lower_size = 2**finished
        upper_size = values.shape[1] // (lower_size * 2**group_bits)
        matrix = hadamard(group_bits)
        if finished == 0:
            shaped = values.reshape(values.shape[0], upper_size, 2**group_bits)
            shaped = jnp.einsum(
                "pak,km->pam",
                shaped,
                matrix,
                precision=lax.Precision.HIGHEST,
                preferred_element_type=jnp.float32,
            )
        else:
            shaped = values.reshape(values.shape[0], upper_size, 2**group_bits, lower_size)
            shaped = jnp.einsum(
                "pakl,km->paml",
                shaped,
                matrix,
                precision=lax.Precision.HIGHEST,
                preferred_element_type=jnp.float32,
            )
        values = shaped.reshape(values.shape[0], -1)
        finished += group_bits
    return values


def rotate_pair(real_part, imag_part, cosine_part, sine_part):
    return (
        real_part * cosine_part - imag_part * sine_part,
        real_part * sine_part + imag_part * cosine_part,
    )


def per_device(
    state_real, state_imag, adjoint_real, adjoint_imag, energies, gamma_angle, beta_angle
):
    local_size = state_real.shape[0]
    local_bits = local_size.bit_length() - 1
    devices = lax.axis_size(("gx", "gy", "gz"))
    global_bits = devices.bit_length() - 1
    row_size = local_size // devices
    row_bits = row_size.bit_length() - 1
    whole_size = local_size * devices
    stacked = jnp.stack([state_real, state_imag, adjoint_real, adjoint_imag])
    transformed = walsh_local(stacked, local_bits)
    exchanged = lax.all_to_all(
        transformed.reshape(4, devices, row_size),
        ("gx", "gy", "gz"),
        split_axis=1,
        concat_axis=1,
        tiled=True,
    )
    outer_matrix = hadamard(global_bits)
    spun_state = jnp.einsum(
        "pnr,nm->pmr",
        exchanged,
        outer_matrix,
        precision=lax.Precision.HIGHEST,
        preferred_element_type=jnp.float32,
    )
    source_ones = count_ones(jnp.arange(devices, dtype=jnp.int32), global_bits)
    row_ones = count_ones(jnp.arange(row_size, dtype=jnp.int32), row_bits)
    device_ones = count_ones(lax.axis_index(("gx", "gy", "gz")), global_bits)
    ones_total = source_ones[:, None] + row_ones[None, :] + device_ones
    eigenvalue = (local_bits + global_bits - 2 * ones_total).astype(jnp.float32)
    beta_part = jnp.sum(
        eigenvalue * (spun_state[2] * spun_state[1] - spun_state[3] * spun_state[0])
    )
    beta_total = lax.psum(beta_part, ("gx", "gy", "gz"))
    angle_beta = beta_angle[0] * eigenvalue
    cosine_part = jnp.cos(angle_beta)
    sine_part = jnp.sin(angle_beta)
    first_re, first_im = rotate_pair(spun_state[0], spun_state[1], cosine_part, sine_part)
    second_re, second_im = rotate_pair(spun_state[2], spun_state[3], cosine_part, sine_part)
    rotated = jnp.stack([first_re, first_im, second_re, second_im])
    unspun = jnp.einsum(
        "pnr,nm->pmr",
        rotated,
        outer_matrix,
        precision=lax.Precision.HIGHEST,
        preferred_element_type=jnp.float32,
    )
    returned = lax.all_to_all(unspun, ("gx", "gy", "gz"), split_axis=1, concat_axis=1, tiled=True)
    middle = walsh_local(returned.reshape(4, local_size), local_bits)
    energy_float = energies.astype(jnp.float32)
    gamma_part = jnp.sum(energy_float * (middle[2] * middle[1] - middle[3] * middle[0]))
    gamma_total = lax.psum(gamma_part, ("gx", "gy", "gz"))
    angle_gamma = gamma_angle[0] * energy_float
    cosine_cost = jnp.cos(angle_gamma)
    sine_cost = jnp.sin(angle_gamma)
    input_real, input_imag = rotate_pair(middle[0], middle[1], cosine_cost, sine_cost)
    adjoint_in_real, adjoint_in_imag = rotate_pair(middle[2], middle[3], cosine_cost, sine_cost)
    gamma_gradient = (gamma_total / whole_size).reshape(1)
    beta_gradient = (beta_total / whole_size).reshape(1)
    return (input_real, input_imag, adjoint_in_real, adjoint_in_imag, gamma_gradient, beta_gradient)


def solution(mesh):
    in_specs = (
        P(("gx", "gy", "gz")),
        P(("gx", "gy", "gz")),
        P(("gx", "gy", "gz")),
        P(("gx", "gy", "gz")),
        P(("gx", "gy", "gz")),
        P(),
        P(),
    )
    out_specs = (
        P(("gx", "gy", "gz")),
        P(("gx", "gy", "gz")),
        P(("gx", "gy", "gz")),
        P(("gx", "gy", "gz")),
        P(),
        P(),
    )
    return jax.shard_map(
        per_device, mesh=mesh, in_specs=in_specs, out_specs=out_specs, check_vma=False
    )
```

profile of v0, /device:TPU:0, one launch (start us, length us, event | category | flops | bytes accessed | tf_op | source)
XLA Modules:
  0.0 199.1 jit_solution(13261115696756516157)
XLA Ops:
  0.6 3.4 %fusion = f32[4,8,128,128]{3,2,1,0:T(8,128)S(1)} fusion(f32[1,8,128,128]{3,2,1,0:T(8,128)} %bitcast.86, f32[1,8,128,128]{3,2,1,0:T(8,128)} %bitcast.87, f32[1,8,128,128]{3,2,1,0:T(8,128)} %bitcast.88, f32[1,8,128,128]{3,2,1,0:T(8,128)} %bitcast.89), kind=kOutput, calls=%fused_computation.4 | convolution fusion | flops 807305216 | bytes 4194304 | tf_op jit(solution)/shard_map/pak,km->pam/dot_general | solution.py:29
  4.1 2.0 convolution_bitcast_fusion.5
  6.0 1.6 reshape.260
  7.6 3.4 %convolution_bitcast_fusion.1 = f32[4,1,8,16384]{3,2,0,1:T(8,128)S(1)} fusion(f32[4,8,16384]{2,1,0:T(8,128)} %reshape.260), kind=kOutput, calls=%fused_computation.1 | convolution fusion | flops 50332544 | bytes 4194304 | tf_op jit(solution)/shard_map/pakl,km->paml/dot_general | solution.py:38
  11.0 1.6 reshape_reshape.2
  12.6 4.3 %copy.17 = f32[4,32,4096]{2,0,1:T(4,128)} copy(f32[4,32,4096]{2,1,0:T(8,128)} %reshape_reshape.2) | data formatting | bytes 4194304 | tf_op jit(solution)/shard_map/reshape;reshape | solution.py:70
  16.9 7.6 %all-to-all-start = ((f32[4,32,4096]{2,0,1:T(4,128)}), f32[4,32,4096]{2,0,1:T(4,128)}, u32[]{:S(2)}, u32[]{:S(2)}) async-start(f32[4,32,4096]{2,0,1:T(4,128)} %copy.17), calls=%async_computation | async-start | bytes 4194304 | tf_op jit(solution)/shard_map/all_to_all | solution.py:69
  25.2 45.9 %all-to-all-done = f32[4,32,4096]{2,0,1:T(4,128)} async-done(((f32[4,32,4096]{2,0,1:T(4,128)}), f32[4,32,4096]{2,0,1:T(4,128)}, u32[]{:S(2)}, u32[]{:S(2)}) %all-to-all-start) | async-done | bytes 2097184 | tf_op jit(solution)/shard_map/all_to_all | solution.py:69
  71.2 4.5 %convolution_bitcast_fusion.3 = f32[4,32,4096]{2,1,0:T(8,128)S(1)} fusion(f32[4,32,4096]{2,0,1:T(4,128)} %all-to-all-done), kind=kOutput, calls=%fused_computation.3 | convolution fusion | flops 201347072 | bytes 4194304 | tf_op jit(solution)/shard_map/pnr,nm->pmr/dot_general | solution.py:77
  75.7 2.3 %multiply_subtract_fusion.3 = (f32[1,32,4096]{2,1,0:T(8,128)S(1)}, f32[1,32,4096]{2,1,0:T(8,128)S(1)}, f32[1,32,4096]{2,1,0:T(8,128)S(1)}, f32[1,32,4096]{2,1,0:T(8,128)S(1)}) fusion(f32[4,32,4096]{2,1,0:T(8,128)S(1)} %convolution_bitcast_fusion.3, s32[]{:T(128)S(6)} %add.365, s32[4096]{0:T(1024)S(1)} %fusion.37, s32[32]{0:T(128)S(1)} %fusion.66, f32[]{:T(128)} %bitcast.81), kind=kLoop, calls=%fused_computation.37 | loop fusion | flops 2359296 | bytes 4210824 | tf_op jit(solution)/shard_map/sub | solution.py:52
  78.0 1.9 convolution_bitcast_fusion.2
  79.9 2.7 %copy.19 = f32[4,32,4096]{2,0,1:T(4,128)} copy(f32[4,32,4096]{2,1,0:T(8,128)S(1)} %convolution_bitcast_fusion.2) | data formatting | bytes 4194304 | tf_op jit(solution)/shard_map/pnr,nm->pmr/transpose | solution.py:99
  82.6 4.9 %all-to-all-start.1 = ((f32[4,32,4096]{2,0,1:T(4,128)}), f32[4,32,4096]{2,0,1:T(4,128)}, u32[]{:S(2)}, u32[]{:S(2)}) async-start(f32[4,32,4096]{2,0,1:T(4,128)} %copy.19), calls=%async_computation.1 | async-start | bytes 4194304 | tf_op jit(solution)/shard_map/all_to_all | solution.py:106
  88.1 0.8 fusion.16
  89.0 45.1 %all-to-all-done.1 = f32[4,32,4096]{2,0,1:T(4,128)} async-done(((f32[4,32,4096]{2,0,1:T(4,128)}), f32[4,32,4096]{2,0,1:T(4,128)}, u32[]{:S(2)}, u32[]{:S(2)}) %all-to-all-start.1) | async-done | bytes 2097184 | tf_op jit(solution)/shard_map/all_to_all | solution.py:106
  134.1 2.8 %copy.20 = f32[4,32,4096]{2,1,0:T(8,128)S(1)} copy(f32[4,32,4096]{2,0,1:T(4,128)} %all-to-all-done.1) | data formatting | bytes 4194304 | tf_op jit(solution)/shard_map/all_to_all | solution.py:106
  136.9 1.5 dot_general.36
  138.4 3.5 %fusion.21 = f32[4,8,128,128]{3,2,1,0:T(8,128)S(1)} fusion(f32[4,8,128,128]{3,2,1,0:T(8,128)} %dot_general.36), kind=kOutput, calls=%fused_computation.55 | convolution fusion | flops 805732352 | bytes 4194304 | tf_op jit(solution)/shard_map/pak,km->pam/dot_general | solution.py:29
  141.9 2.0 convolution_bitcast_fusion.4
  143.9 1.6 reshape.261
  145.5 3.4 %convolution_bitcast_fusion = f32[4,1,8,16384]{3,2,0,1:T(8,128)S(1)} fusion(f32[4,8,16384]{2,1,0:T(8,128)} %reshape.261), kind=kOutput, calls=%fused_computation | convolution fusion | flops 50332544 | bytes 4194304 | tf_op jit(solution)/shard_map/pakl,km->paml/dot_general | solution.py:38
  149.5 0.6 copy-done
  150.0 3.7 %multiply_reduce_fusion = (f32[]{:T(128)}, f32[131072]{0:T(1024)}, f32[131072]{0:T(1024)}, f32[131072]{0:T(1024)}, f32[131072]{0:T(1024)}) fusion(f32[131072]{0:T(1024)S(1)} %bitcast.83, f32[131072]{0:T(1024)S(1)} %bitcast.85, f32[131072]{0:T(1024)S(1)} %bitcast.82, f32[131072]{0:T(1024)S(1)} %bitcast.84, s32[131072]{0:T(1024)S(1)} %copy-done, f32[]{:T(128)} %bitcast.80), kind=kLoop, calls=%fused_computation.28 | loop fusion | flops 2490367 | bytes 4718600 | tf_op jit(solution)/shard_map/reduce_sum | solution.py:109
  153.8 41.7 %all-reduce = (f32[]{:T(128)}, f32[]{:T(128)}) all-reduce(f32[]{:T(128)} %get-tuple-element.16, f32[]{:T(128)} %fusion.16), channel_id=1, replica_groups=mesh['gx'=2,'gy'=4,'gz'=4] {'gx','gy','gz'}, use_global_device_ids=true, to_apply=%region_1.0 | all-reduce | flops 2 | bytes 16 | tf_op jit(solution)/shard_map/psum | solution.py:110
  (8 shorter events, 0.6 us)
Async XLA Ops:
  16.9 54.2 %all-to-all-start = ((f32[4,32,4096]{2,0,1:T(4,128)}), f32[4,32,4096]{2,0,1:T(4,128)}, u32[]{:S(2)}, u32[]{:S(2)}) async-start(f32[4,32,4096]{2,0,1:T(4,128)} %copy.17), calls=%async_computation | async-start | bytes 4194304 | tf_op jit(solution)/shard_map/all_to_all | solution.py:69
  82.6 51.5 %all-to-all-start.1 = ((f32[4,32,4096]{2,0,1:T(4,128)}), f32[4,32,4096]{2,0,1:T(4,128)}, u32[]{:S(2)}, u32[]{:S(2)}) async-start(f32[4,32,4096]{2,0,1:T(4,128)} %copy.19), calls=%async_computation.1 | async-start | bytes 4194304 | tf_op jit(solution)/shard_map/all_to_all | solution.py:106
  149.0 1.0 copy-start
where the time goes:
time: 200 us; the launch traced here: 199 us
  waiting for transfers between devices  91 us (46%)
  blocking collectives  41.7 us (21%)
  matrix products  24.1 us (12%)
  local copies, waits for them, and re-layouts  17.2 us (9%)
  starting transfers between devices  12.5 us (6%)
  other arithmetic  6.94 us (3%)
  between operations  5.65 us (3%)
    all_to_all x1, waiting for transfers between devices, per_device(): lax.all_to_all(transformed.reshape(4, devices, row_size), ('gx', 'gy', 'g...  45.9 us
    all_to_all x1, waiting for transfers between devices, per_device(): lax.all_to_all(unspun, ('gx', 'gy', 'gz'), split_axis=1, concat_axis=1, t...  45.1 us
    psum x1, blocking collectives, per_device(): gamma_total = lax.psum(gamma_part, ('gx', 'gy', 'gz'))  41.7 us
    dot_general x4, matrix products, walsh_local(): jnp.einsum('pakl,km->paml', shaped, matrix, precision=lax.Precision.HIGHE...  10.7 us
    all_to_all x1, starting transfers between devices, per_device(): lax.all_to_all(transformed.reshape(4, devices, row_size), ('gx', 'gy', 'g...  7.6 us
    dot_general x2, matrix products, walsh_local(): jnp.einsum('pak,km->pam', shaped, matrix, precision=lax.Precision.HIGHEST...  6.94 us
    another operation x2, local copies, waits for them, and re-layouts, per_device(): transformed.reshape(4, devices, row_size)  5.91 us
    all_to_all x1, starting transfers between devices, per_device(): lax.all_to_all(unspun, ('gx', 'gy', 'gz'), split_axis=1, concat_axis=1, t...  4.91 us
  transfers between devices with their start and end apart: 2, of which 2 were waited for; matrix products, arithmetic and copies ran while one was open for 0% of the time, Pallas kernels for 0%

commit v1 on v0

v1 whole, which is shorter than its diff:
```python
import functools

import jax
import jax.numpy as jnp
import numpy as np
from jax import lax
from jax.experimental import pallas as pl
from jax.experimental.pallas import tpu as pltpu
from jax.sharding import PartitionSpec as P

AXES = ("gx", "gy", "gz")
LANES = 128
SUB = 8
VMEM_BYTES = 12 * 1024 * 1024
MID_VMEM_BYTES = 24 * 1024 * 1024
LARGE_VMEM_BYTES = 60 * 1024 * 1024


def sin_cos(angle):
    turns = jnp.round(angle * 0.6366197723675814)
    rest = angle - turns * 1.5703125
    rest = rest - turns * 4.837512969970703125e-4
    rest = rest - turns * 7.54978995489188216e-8
    square = rest * rest
    sine = (-1.9515295891e-4 * square + 8.3321608736e-3) * square - 1.6666654611e-1
    sine = rest + rest * square * sine
    cosine = (2.443315711809948e-5 * square - 1.388731625493765e-3) * square
    cosine = 1.0 - 0.5 * square + square * square * (cosine + 4.166664568298827e-2)
    quadrant = turns.astype(jnp.int32) & 3
    swap = (quadrant & 1) == 1
    sine, cosine = jnp.where(swap, cosine, sine), jnp.where(swap, sine, cosine)
    sine = jnp.where(quadrant >= 2, -sine, sine)
    cosine = jnp.where((quadrant == 1) | (quadrant == 2), -cosine, cosine)
    return sine, cosine


def splat(number_ref):
    return jnp.full((SUB, LANES), number_ref[0], jnp.float32)


def split_in_two(values):
    high = values.astype(jnp.bfloat16)
    return high, (values - high.astype(jnp.float32)).astype(jnp.bfloat16)


def flip_sublane(tiles, bit):
    if 2 * bit == SUB:
        return pltpu.roll(tiles, bit, 1)
    row = lax.broadcasted_iota(jnp.int32, tiles.shape, 1)
    return jnp.where(
        (row & bit) == 0, pltpu.roll(tiles, SUB - bit, 1), pltpu.roll(tiles, bit, 1)
    )


def rotate_leading(load, store, count, tangent, group_bits=3):
    finished = 0
    total = count.bit_length() - 1
    while finished < total:
        width = min(group_bits, total - finished)
        stride = 1 << finished
        size = 1 << width
        for base in range(count):
            if base & (stride * (size - 1)):
                continue
            items = [load(base + stride * pos, finished > 0) for pos in range(size)]
            for bit_pos in range(width):
                bit = 1 << bit_pos
                items = [
                    (
                        items[pos][0] - tangent * items[pos ^ bit][1],
                        items[pos][1] + tangent * items[pos ^ bit][0],
                    )
                    for pos in range(size)
                ]
            for pos in range(size):
                store(base + stride * pos, items[pos])
        finished += width


def pre_kernel(
    beta_ref, sr_ref, si_ref, ar_ref, ai_ref, out_ref, held, turned, in_sem, out_sem
):
    count, rows, _ = sr_ref.shape
    tiles = rows // SUB
    sources = (sr_ref, si_ref, ar_ref, ai_ref)

    def fetch(tile, part):
        return pltpu.make_async_copy(
            sources[part].at[:, pl.ds(tile * SUB, SUB), :],
            held.at[tile, part],
            in_sem.at[tile, part],
        )

    def write(tile, pair):
        return pltpu.make_async_copy(
            turned.at[tile, pair],
            out_ref.at[:, pl.ds(2 * pair, 2), pl.ds(tile * SUB, SUB), :],
            out_sem.at[tile, pair],
        )

    for tile in range(tiles):
        for part in range(4):
            fetch(tile, part).start()
    sine, cosine = sin_cos(splat(beta_ref))
    tangent = sine / cosine
    for tile in range(tiles):
        for pair in range(2):
            for part in range(2):
                fetch(tile, 2 * pair + part).wait()

            def load(pos, again):
                if again:
                    return turned[tile, pair, pos, 0], turned[tile, pair, pos, 1]
                return held[tile, 2 * pair, pos], held[tile, 2 * pair + 1, pos]

            def store(pos, item):
                turned[tile, pair, pos, 0] = item[0]
                turned[tile, pair, pos, 1] = item[1]

            rotate_leading(load, store, count, tangent)
            write(tile, pair).start()
    for tile in range(tiles):
        for pair in range(2):
            write(tile, pair).wait()


def pre_rotate(beta, sr, si, ar, ai):
    count, rows, _ = sr.shape
    tiles = rows // SUB
    hbm = pl.BlockSpec(memory_space=pltpu.HBM)
    size = count * rows * LANES
    return pl.pallas_call(
        pre_kernel,
        in_specs=[pl.BlockSpec(memory_space=pltpu.SMEM)] + [hbm] * 4,
        out_specs=hbm,
        out_shape=jax.ShapeDtypeStruct((count, 4, rows, LANES), jnp.float32),
        scratch_shapes=[
            pltpu.VMEM((tiles, 4, count, SUB, LANES), jnp.float32),
            pltpu.VMEM((tiles, 2, count, 2, SUB, LANES), jnp.float32),
            pltpu.SemaphoreType.DMA((tiles, 4)),
            pltpu.SemaphoreType.DMA((tiles, 2)),
        ],
        compiler_params=pltpu.CompilerParams(vmem_limit_bytes=LARGE_VMEM_BYTES),
        cost_estimate=pl.CostEstimate(
            flops=size * 40, bytes_accessed=size * 32, transcendentals=0
        ),
        name="rotate_top",
    )(beta, sr, si, ar, ai)


def prep_kernel(
    qubits, beta_ref, gamma_ref, energy_ref, matrix_ref, tangent_ref, phase_ref, found_ref
):
    sine, cosine = sin_cos(splat(beta_ref))
    tangent_ref[...] = sine / cosine
    sine, cosine = sine[:1], cosine[:1]
    scale = jnp.ones_like(cosine)
    for _ in range(qubits - 7):
        scale = scale * cosine
    powers = []
    for ones in range(8):
        value = scale
        for _ in range(7 - ones):
            value = value * cosine
        for _ in range(ones):
            value = value * sine
        powers.append(-value if ones & 2 else value)
    row = lax.broadcasted_iota(jnp.int32, (LANES, LANES), 0)
    column = lax.broadcasted_iota(jnp.int32, (LANES, LANES), 1)
    ones = lax.population_count(row ^ column)
    real_part = jnp.zeros((LANES, LANES), jnp.float32)
    imag_part = jnp.zeros((LANES, LANES), jnp.float32)
    for number in range(8):
        if number & 1:
            imag_part = jnp.where(ones == number, powers[number], imag_part)
        else:
            real_part = jnp.where(ones == number, powers[number], real_part)
    real_high, real_low = split_in_two(real_part)
    imag_high, imag_low = split_in_two(imag_part)
    for place, real_term, imag_term in (
        (0, real_high, imag_high),
        (1, real_high, imag_high),
        (2, real_low, imag_low),
    ):
        upper = pl.ds(2 * LANES * place, LANES)
        lower = pl.ds(2 * LANES * place + LANES, LANES)
        matrix_ref[upper, :LANES] = real_term
        matrix_ref[upper, LANES:] = imag_term
        matrix_ref[lower, :LANES] = -imag_term
        matrix_ref[lower, LANES:] = real_term

    local_size = energy_ref.shape[0] * LANES
    tiles = 4 * SUB
    gamma = gamma_ref[0]

    def step(pos, best):
        rows = pl.ds(pl.multiple_of(pos * tiles, tiles), tiles)
        energy = energy_ref[rows, :]
        index = (
            lax.broadcasted_iota(jnp.int32, energy.shape, 0) * LANES
            + lax.broadcasted_iota(jnp.int32, energy.shape, 1)
            + pos * (tiles * LANES)
        )
        sine_part, cosine_part = sin_cos(gamma * energy.astype(jnp.float32))
        phase_ref[0, rows, :] = cosine_part
        phase_ref[1, rows, :] = sine_part
        return jnp.maximum(best, energy * local_size + index)

    best = lax.fori_loop(
        0, energy_ref.shape[0] // tiles, step, jnp.zeros((tiles, LANES), jnp.int32)
    )
    found_ref[...] = jnp.max(best.reshape(-1, SUB, LANES), axis=0)


def prepare(qubits, beta, gamma, energies):
    rows = energies.shape[0]
    smem = pl.BlockSpec(memory_space=pltpu.SMEM)
    vmem = pl.BlockSpec(memory_space=pltpu.VMEM)
    return pl.pallas_call(
        functools.partial(prep_kernel, qubits),
        in_specs=[smem, smem, vmem],
        out_specs=[vmem] * 4,
        out_shape=[
            jax.ShapeDtypeStruct((6 * LANES, 2 * LANES), jnp.bfloat16),
            jax.ShapeDtypeStruct((SUB, LANES), jnp.float32),
            jax.ShapeDtypeStruct((2, rows, LANES), jnp.float32),
            jax.ShapeDtypeStruct((SUB, LANES), jnp.int32),
        ],
        compiler_params=pltpu.CompilerParams(vmem_limit_bytes=VMEM_BYTES),
        cost_estimate=pl.CostEstimate(
            flops=rows * LANES * 50, bytes_accessed=rows * LANES * 12, transcendentals=0
        ),
        name="phases",
    )(beta, gamma, energies)


def labs_energy(spins, qubits, count_ones):
    energy = 0
    for lag in range(1, qubits):
        span = qubits - lag
        differ = count_ones((spins ^ (spins >> lag)) & ((1 << span) - 1))
        correlation = span - 2 * differ
        energy = energy + correlation * correlation
    return energy


@functools.lru_cache(maxsize=None)
def highest_table(qubits, local_bits):
    every = 2**qubits - 1
    second = sum(2**place for place in range(0, qubits, 2))
    same = [value >> local_bits for value in (0, every, second, every ^ second)]
    low = np.arange(2**local_bits, dtype=np.int32)
    table, covered = {}, set()
    for top in range(2 ** (qubits - local_bits)):
        if top in covered:
            continue
        covered.update(top ^ value for value in same)
        energy = labs_energy(
            low | np.int32(top << local_bits),
            qubits,
            lambda bits: np.bitwise_count(bits).astype(np.int32),
        )
        highest = int(energy.max())
        places = np.flatnonzero(energy == highest)
        if highest in table or len(places) > 1:
            return None
        table[highest] = (top << local_bits) | int(places[0])
    return table


def energy_kernel(qubits, table, found_ref, out_ref):
    count, rows, _ = out_ref.shape
    block = rows * LANES
    local_bits = (count * block).bit_length() - 1
    found = found_ref[...]
    device = lax.axis_index(AXES)
    if table is None:
        mask = found
    else:
        for shift in (1, 2, 4):
            found = jnp.maximum(found, pltpu.roll(found, shift, 0))
        for shift in (1, 2, 4, 8, 16, 32, 64):
            found = jnp.maximum(found, pltpu.roll(found, shift, 1))
        highest = found >> local_bits
        mask = (found & ((1 << local_bits) - 1)) + (device << local_bits)
        for value, index in table.items():
            mask = jnp.where(highest == value, mask ^ index, mask)
    offset = (
        lax.broadcasted_iota(jnp.int32, (SUB, LANES), 0) * LANES
        + lax.broadcasted_iota(jnp.int32, (SUB, LANES), 1)
    ) ^ mask
    tiles = rows // SUB

    def step(pos, carry):
        for tile in range(tiles):
            place = (pos << local_bits) + device * block + tile * (SUB * LANES)
            spins = offset ^ place
            energy = jnp.zeros((SUB, LANES), jnp.float32)
            for lag in range(1, qubits):
                span = qubits - lag
                differ = lax.population_count((spins ^ (spins >> lag)) & ((1 << span) - 1))
                correlation = (span - 2 * differ).astype(jnp.float32)
                energy = energy + correlation * correlation
            out_ref[pos, pl.ds(tile * SUB, SUB), :] = energy
        return carry

    lax.fori_loop(0, count, step, 0)


def exchanged_energies(qubits, shape, found):
    local_bits = (shape[0] * shape[1] * shape[2]).bit_length() - 1
    table = highest_table(qubits, local_bits)
    if table is None:
        highest = sum(span * span for span in range(1, qubits))
        index = (found & ((1 << local_bits) - 1)) + (lax.axis_index(AXES) << local_bits)
        index = jnp.max(jnp.where(found >> local_bits == highest, index, -1))
        found = jnp.full((SUB, LANES), lax.pmax(index, AXES), jnp.int32)
    vmem = pl.BlockSpec(memory_space=pltpu.VMEM)
    return pl.pallas_call(
        functools.partial(energy_kernel, qubits, table),
        in_specs=[vmem],
        out_specs=vmem,
        out_shape=jax.ShapeDtypeStruct(shape, jnp.float32),
        compiler_params=pltpu.CompilerParams(vmem_limit_bytes=VMEM_BYTES),
        cost_estimate=pl.CostEstimate(
            flops=(200 << local_bits), bytes_accessed=(4 << local_bits), transcendentals=0
        ),
        name="energies",
    )(found)


def tile_place(place, number, tiles):
    first = (place * (tiles * SUB + 1) + SUB - 1) // SUB
    if number == tiles - 1 and place % SUB not in (0, SUB - 1):
        return None, (first - 1, first + tiles - 1)
    return first + number, None


def shared_tile(place, tiles):
    return ((place + 1) * (tiles * SUB + 1) - 1) // SUB


def mid_kernel(
    tangent_ref, matrix_ref, slope_ref, energy_ref, in_ref, out_ref, split, wide, edge
):
    count, rows, _ = energy_ref.shape
    tiles = rows // SUB
    tangent = tangent_ref[...]
    span = max(1, 64 // rows)

    def rows_step(pos, carry):
        some = pl.ds(pos * span, span)
        there = pl.ds(pl.multiple_of(pos * (span * rows), span * rows), span * rows)
        for pair_pos in range(2):
            pair = [
                in_ref[some, pl.ds((2 * pair_pos + part) * rows, rows), :].reshape(
                    span, tiles, SUB, LANES
                )
                for part in range(2)
            ]
            bit = 1
            while bit < tiles:
                other = [
                    jnp.concatenate(
                        [part[:, tile ^ bit : (tile ^ bit) + 1] for tile in range(tiles)], axis=1
                    )
                    for part in pair
                ]
                pair = [pair[0] - tangent * other[1], pair[1] + tangent * other[0]]
                bit *= 2
            pair = [part.reshape(span * tiles, SUB, LANES) for part in pair]
            for bit in (1, 2, 4):
                other = [flip_sublane(part, bit) for part in pair]
                pair = [pair[0] - tangent * other[1], pair[1] + tangent * other[0]]
            for part in range(2):
                first, second = split_in_two(pair[part].reshape(span * rows, LANES))
                for place, term in ((0, first), (1, second), (2, first)):
                    start = (2 * place + part) * LANES
                    split[pair_pos, there, start : start + LANES] = term
        return carry

    lax.fori_loop(0, count // span, rows_step, 0)
    half = count * rows // 2
    for pair_pos in range(2):
        for pos in range(2):
            there = pl.ds(pos * half, half)
            wide[pair_pos, there, :] = jnp.dot(
                split[pair_pos, there, :], matrix_ref[...], preferred_element_type=jnp.float32
            )

    def group(tile, bits, places):
        pairs = []
        for pair_pos in range(2):
            items = []
            for place in places:
                here = pl.ds(place * rows + tile * SUB, SUB)
                items.append([wide[pair_pos, here, :LANES], wide[pair_pos, here, LANES:]])
            for bit_pos in range(bits):
                bit = 1 << bit_pos
                items = [
                    (
                        items[pos][0] - tangent * items[pos ^ bit][1],
                        items[pos][1] + tangent * items[pos ^ bit][0],
                    )
                    for pos in range(len(places))
                ]
            pairs.append(items)
        state, adjoint = pairs
        share = 0.0
        for pos in range(len(places)):
            flipped = [
                functools.reduce(
                    jnp.add, [state[pos ^ (1 << bit)][part] for bit in range(bits)]
                )
                for part in range(2)
            ]
            share = share + (adjoint[pos][0] * flipped[1] - adjoint[pos][1] * flipped[0])
        return pairs, share

    beta_sum = slope_ref[...]
    gamma_sum = jnp.zeros((SUB, LANES), jnp.float32)
    total_bits = count.bit_length() - 1
    last_bits = min(3, total_bits)
    finished, left = last_bits, total_bits
    while finished < total_bits:
        bits = min(3, total_bits - finished)
        left -= bits
        stride = 1 << finished
        total = jnp.zeros((SUB, LANES), jnp.float32)
        for tile in range(tiles):
            for base in range(count):
                if base & (stride * ((1 << bits) - 1)):
                    continue
                places = [base + stride * pos for pos in range(1 << bits)]
                pairs, share = group(tile, bits, places)
                total = total + share
                for pair_pos, items in enumerate(pairs):
                    for place, item in zip(places, items):
                        here = pl.ds(place * rows + tile * SUB, SUB)
                        wide[pair_pos, here, :LANES] = item[0]
                        wide[pair_pos, here, LANES:] = item[1]
        for _ in range(left):
            total = total * (1.0 + tangent * tangent)
        beta_sum = beta_sum + total
        finished += bits

    block_tiles = 4 * tiles
    for base in range(0, count, 1 << last_bits):
        places = range(base, base + (1 << last_bits))
        for tile in range(tiles):
            pairs, share = group(tile, last_bits, places)
            state, adjoint = pairs
            beta_sum = beta_sum + share
            for pos, place in enumerate(places):
                value = adjoint[pos][0] * state[pos][1] - adjoint[pos][1] * state[pos][0]
                energy = energy_ref[place, pl.ds(tile * SUB, SUB), :]
                gamma_sum = gamma_sum + energy * value
                for part in range(4):
                    item = pairs[part // 2][pos][part % 2]
                    whole, halves = tile_place(place, part * tiles + tile, block_tiles)
                    if halves:
                        edge[place] = item
                    else:
                        out_ref[pl.ds(whole * SUB, SUB), :] = item

    beta_row = jnp.sum(beta_sum, axis=0, keepdims=True)
    gamma_row = jnp.sum(gamma_sum, axis=0, keepdims=True)
    half_lanes = LANES // 2
    lane = lax.broadcasted_iota(jnp.int32, (1, LANES), 1)
    value = jnp.where(
        lane < half_lanes,
        beta_row + pltpu.roll(beta_row, half_lanes, 1),
        gamma_row + pltpu.roll(gamma_row, half_lanes, 1),
    )
    value = jnp.broadcast_to(value, (SUB, LANES))
    row = lax.broadcasted_iota(jnp.int32, (SUB, LANES), 0)
    for place in range(count):
        sublane = place % SUB
        if sublane == SUB - 1:
            continue
        tile = value
        if 0 < sublane:
            tile = jnp.where(row < sublane, edge[place], tile)
        if sublane < SUB - 2:
            tile = jnp.where(row > sublane, edge[place + 1], tile)
        out_ref[pl.ds(shared_tile(place, block_tiles) * SUB, SUB), :] = tile


def mid_rotate(tangent, matrix, slope, energies, received):
    count, rows, _ = energies.shape
    size = received.size
    flat = (2, count * rows)
    out_shape = (count * (4 * rows + 1), LANES)
    vmem = pl.BlockSpec(memory_space=pltpu.VMEM)
    return pl.pallas_call(
        mid_kernel,
        in_specs=[vmem] * 5,
        out_specs=vmem,
        out_shape=jax.ShapeDtypeStruct(out_shape, jnp.float32),
        scratch_shapes=[
            pltpu.VMEM(flat + (6 * LANES,), jnp.bfloat16),
            pltpu.VMEM(flat + (2 * LANES,), jnp.float32),
            pltpu.VMEM((count, SUB, LANES), jnp.float32),
        ],
        compiler_params=pltpu.CompilerParams(vmem_limit_bytes=MID_VMEM_BYTES),
        cost_estimate=pl.CostEstimate(
            flops=size * 2 * 256 * 3, bytes_accessed=size * 8, transcendentals=0
        ),
        name="rotate_rest",
    )(tangent, matrix, slope, energies, received)


def slope_kernel(sr_ref, si_ref, ar_ref, ai_ref, out_ref):
    count, rows, _ = sr_ref.shape
    tiles = rows // SUB
    row = lax.broadcasted_iota(jnp.int32, (LANES, LANES), 0)
    column = lax.broadcasted_iota(jnp.int32, (LANES, LANES), 1)
    flips = (lax.population_count(row ^ column) == 1).astype(jnp.float32)

    def step(pos, total):
        def flipped(ref):
            own = ref[pos]
            near = own.reshape(tiles, SUB, LANES)
            result = jnp.dot(
                own,
                flips,
                precision=lax.Precision.HIGHEST,
                preferred_element_type=jnp.float32,
            ).reshape(tiles, SUB, LANES)
            for bit in (1, 2, 4):
                result = result + flip_sublane(near, bit)
            bit = 1
            while bit < tiles:
                result = result + jnp.concatenate(
                    [near[tile ^ bit : (tile ^ bit) + 1] for tile in range(tiles)], axis=0
                )
                bit *= 2
            bit = 1
            while bit < count:
                result = result + ref[pos ^ bit].reshape(tiles, SUB, LANES)
                bit *= 2
            return result

        real_part, imag_part = flipped(sr_ref), flipped(si_ref)
        adjoint_real = ar_ref[pos].reshape(tiles, SUB, LANES)
        adjoint_imag = ai_ref[pos].reshape(tiles, SUB, LANES)
        part = adjoint_real * imag_part - adjoint_imag * real_part
        return total + jnp.sum(part, axis=0)

    out_ref[...] = lax.fori_loop(0, count, step, jnp.zeros((SUB, LANES), jnp.float32))


def local_slope(sr, si, ar, ai):
    vmem = pl.BlockSpec(memory_space=pltpu.VMEM)
    return pl.pallas_call(
        slope_kernel,
        in_specs=[vmem] * 4,
        out_specs=vmem,
        out_shape=jax.ShapeDtypeStruct((SUB, LANES), jnp.float32),
        compiler_params=pltpu.CompilerParams(vmem_limit_bytes=VMEM_BYTES),
        cost_estimate=pl.CostEstimate(
            flops=sr.size * 2 * 2 * LANES * 6, bytes_accessed=sr.size * 16, transcendentals=0
        ),
        name="local_slope",
    )(sr, si, ar, ai)


def last_kernel(whole_size, phase_ref, in_ref, *refs):
    out_refs, (gamma_ref, beta_ref, done, out_sem) = refs[:4], refs[4:]
    _, count, rows, _ = phase_ref.shape
    parts = out_sem.shape[0]
    share = count // parts
    tiles = rows // SUB
    row = lax.broadcasted_iota(jnp.int32, (SUB, LANES), 0)

    def write(pos, place):
        some = pl.ds(pos * share, share)
        return pltpu.make_async_copy(
            done.at[place, some], out_refs[place].at[some], out_sem.at[pos, place]
        )

    sublane = lax.axis_index(AXES) & (SUB - 1)
    skip = (SUB - sublane) & (SUB - 1)
    below = jnp.where(sublane == SUB - 1, SUB, sublane)
    block_tiles = 4 * tiles
    block = block_tiles * SUB + 1

    def load(pos, number):
        start = pos * block
        if number < block_tiles - 1:
            return in_ref[pl.ds(start + skip + number * SUB, SUB), :]
        first = pltpu.roll(in_ref[pl.ds(start, SUB), :], sublane, 0)
        last = in_ref[pl.ds(start + block - SUB, SUB), :]
        last = pltpu.roll(last, (sublane + 1) & (SUB - 1), 0)
        whole = in_ref[pl.ds(start + block - 1 - SUB, SUB), :]
        return jnp.where(sublane == 0, whole, jnp.where(row < below, last, first))

    for part in range(parts):
        for pos in range(part * share, (part + 1) * share):
            for tile in range(tiles):
                here = pl.ds(tile * SUB, SUB)
                cosine, sine = phase_ref[0, pos, here], phase_ref[1, pos, here]
                sr, si, ar, ai = (load(pos, place * tiles + tile) for place in range(4))
                done[0, pos, here] = sr * cosine - si * sine
                done[1, pos, here] = sr * sine + si * cosine
                done[2, pos, here] = ar * cosine - ai * sine
                done[3, pos, here] = ar * sine + ai * cosine
        for place in range(4):
            write(part, place).start()
    extra = jnp.where(sublane == SUB - 1, 0, block - 1)
    total = in_ref[pl.ds(extra, 1), :]
    for pos in range(1, count):
        total = total + in_ref[pl.ds(pos * block + extra, 1), :]
    first = lax.broadcasted_iota(jnp.int32, (1, LANES), 1) < LANES // 2
    beta_ref[...] = jnp.sum(jnp.where(first, total, 0.0), axis=1, keepdims=True) / whole_size
    gamma_ref[...] = jnp.sum(jnp.where(first, 0.0, total), axis=1, keepdims=True) / whole_size
    for part in range(parts):
        for place in range(4):
            write(part, place).wait()


def last_phase(whole_size, phase, returned):
    _, count, rows, _ = phase.shape
    parts = 4
    shape = jax.ShapeDtypeStruct((count, rows, LANES), jnp.float32)
    number = jax.ShapeDtypeStruct((1, 1), jnp.float32)
    vmem = pl.BlockSpec(memory_space=pltpu.VMEM)
    hbm = pl.BlockSpec(memory_space=pltpu.HBM)
    return pl.pallas_call(
        functools.partial(last_kernel, whole_size),
        in_specs=[vmem] * 2,
        out_specs=[hbm] * 4 + [vmem] * 2,
        out_shape=[shape] * 4 + [number] * 2,
        scratch_shapes=[
            pltpu.VMEM((4, count, rows, LANES), jnp.float32),
            pltpu.SemaphoreType.DMA((parts, 4)),
        ],
        compiler_params=pltpu.CompilerParams(vmem_limit_bytes=VMEM_BYTES),
        cost_estimate=pl.CostEstimate(
            flops=returned.size * 3, bytes_accessed=returned.size * 10, transcendentals=0
        ),
        name="cost_phase",
    )(phase, returned)


def swap(values):
    return lax.all_to_all(values, AXES, split_axis=0, concat_axis=0, tiled=True)


def per_device(
    state_real, state_imag, adjoint_real, adjoint_imag, energies, gamma_angle, beta_angle
):
    local_size = state_real.shape[0]
    devices = lax.axis_size(AXES)
    whole_size = local_size * devices
    qubits = whole_size.bit_length() - 1
    shape = (devices, local_size // (devices * LANES), LANES)
    arrays = [
        part.reshape(shape) for part in (state_real, state_imag, adjoint_real, adjoint_imag)
    ]
    there = swap(pre_rotate(beta_angle, *arrays)).reshape(devices, -1, LANES)
    matrix, tangent, phase, found = prepare(
        qubits, beta_angle, gamma_angle, energies.reshape(-1, LANES)
    )
    elsewhere = exchanged_energies(qubits, shape, found)
    slope = local_slope(*arrays)
    middle = mid_rotate(tangent, matrix, slope, elsewhere, there)
    back = swap(middle.reshape(devices, -1, 1, LANES)).reshape(middle.shape)
    *outputs, gamma_gradient, beta_gradient = last_phase(
        whole_size, phase.reshape((2,) + shape), back
    )
    return tuple(part.reshape(-1) for part in outputs) + (
        gamma_gradient.reshape(1),
        beta_gradient.reshape(1),
    )


def solution(mesh):
    in_specs = (P(AXES),) * 5 + (P(), P())
    out_specs = (P(AXES),) * 4 + (P(), P())
    return jax.shard_map(
        per_device, mesh=mesh, in_specs=in_specs, out_specs=out_specs, check_vma=False
    )
```

time: 200 us -> 119 us (0.59)
  waiting for transfers between devices: 91 us -> 29.5 us
  matrix products: 24.1 us -> 0 us
  Pallas kernels: 0 us -> 20.9 us
  blocking collectives: 41.7 us -> 55.2 us
  local copies, waits for them, and re-layouts: 17.2 us -> 4.12 us
  other arithmetic: 6.94 us -> 0 us
  starting transfers between devices: 12.5 us -> 7.3 us
  between operations: 5.65 us -> 2.03 us
    all_to_all x2 -> x1, waiting for transfers between devices: 91 us -> 29.5 us  [swap(): return lax.all_to_all(values, AXES, split_axis=0, concat_axis=0, tiled=True)]
    all_to_all x0 -> x1, blocking collectives: none -> 55.2 us  [swap(): return lax.all_to_all(values, AXES, split_axis=0, concat_axis=0, tiled=True)]
    psum x1 -> x0, blocking collectives: 41.7 us -> none  [per_device(): gamma_total = lax.psum(gamma_part, ('gx', 'gy', 'gz'))]
    dot_general x8 -> x0, matrix products: 24.1 us -> none  [the longest x4 10.7 us: walsh_local(): jnp.einsum('pakl,km->paml', shaped, matrix, precision=lax.Precision.HIGHE...]
    pallas_call x0 -> x6, Pallas kernels: none -> 20.9 us  [the longest x1 7.56 us: local_slope(): pl.pallas_call(slope_kernel, in_specs=[vmem] * 4, out_specs=vmem, out_sha...]
    another operation x3 -> x0, local copies, waits for them, and re-layouts: 7.46 us -> none  [the longest x2 5.91 us: per_device(): transformed.reshape(4, devices, row_size)]
    all_to_all x2 -> x1, starting transfers between devices: 12.5 us -> 7.3 us  [swap(): return lax.all_to_all(values, AXES, split_axis=0, concat_axis=0, tiled=True)]
    reduce_sum x2 -> x0, other arithmetic: 4.59 us -> none  [the longest x1 3.74 us: per_device(): jnp.sum(energy_float * (middle[2] * middle[1] - middle[3] * middle[0]))]
  transfers between devices with their start and end apart: 2 -> 1, of which waited for: 2 -> 1; matrix products, arithmetic and copies ran while one was open for 0% -> 0% of each run, Pallas kernels for 0% -> 11%
where the time goes in v1:
time: 119 us
  blocking collectives  55.2 us (46%)
  waiting for transfers between devices  29.5 us (25%)
  Pallas kernels  20.9 us (18%)
  starting transfers between devices  7.3 us (6%)
  local copies, waits for them, and re-layouts  4.12 us (3%)
  between operations  2.03 us (2%)
    all_to_all x1, blocking collectives, swap(): return lax.all_to_all(values, AXES, split_axis=0, concat_axis=0, tiled=True)  55.2 us
    all_to_all x1, waiting for transfers between devices, swap(): return lax.all_to_all(values, AXES, split_axis=0, concat_axis=0, tiled=True)  29.5 us
    pallas_call x1, Pallas kernels, local_slope(): pl.pallas_call(slope_kernel, in_specs=[vmem] * 4, out_specs=vmem, out_sha...  7.56 us
    all_to_all x1, starting transfers between devices, swap(): return lax.all_to_all(values, AXES, split_axis=0, concat_axis=0, tiled=True)  7.3 us
    unnamed x14, local copies, waits for them, and re-layouts  4.12 us
    pallas_call x1, Pallas kernels, exchanged_energies(): pl.pallas_call(functools.partial(energy_kernel, qubits, table), in_specs=...  3.91 us
    pallas_call x1, Pallas kernels, mid_rotate(): pl.pallas_call(mid_kernel, in_specs=[vmem] * 5, out_specs=vmem, out_shape...  3.63 us
    pallas_call x1, Pallas kernels, pre_rotate(): pl.pallas_call(pre_kernel, in_specs=[pl.BlockSpec(memory_space=pltpu.SMEM...  2.73 us
  transfers between devices with their start and end apart: 1, of which 1 were waited for; matrix products, arithmetic and copies ran while one was open for 0% of the time, Pallas kernels for 11%

profile of v1, /device:TPU:0, one launch (start us, length us, event | category | flops | bytes accessed | tf_op | source)
XLA Modules:
  0.0 119.0 jit_solution(12506946516684847129)
XLA Ops:
  1.3 2.7 %rotate_top.1 = f32[32,4,32,128]{3,2,1,0:T(8,128)} custom-call(f32[1]{0:T(128)S(6)} %copy.15.beta_ref, f32[32,32,128]{2,1,0:T(8,128)} %bitcast.18, f32[32,32,128]{2,1,0:T(8,128)} %bitcast.20, f32[32,32,128]{2,1,0:T(8,128)} %bitcast.22, f32[32,32,128]{2,1,0:T(8,128)} %bitcast.24), custom_call_target="tpu_custom_call" | custom-call | flops 5242880 | bytes 4194304 | tf_op jit(solution)/shard_map/rotate_top/pallas_call | solution.py:132
  4.0 0.0 copy-start.6
  4.0 0.0 copy-start
  4.0 7.3 %all-to-all-start = ((f32[32,4,32,128]{3,2,1,0:T(8,128)}), f32[32,4,32,128]{3,2,1,0:T(8,128)S(1)}, u32[]{:S(2)}, u32[]{:S(2)}) async-start(f32[32,4,32,128]{3,2,1,0:T(8,128)} %rotate_top.1), calls=%async_computation | async-start | bytes 4194304 | tf_op jit(solution)/shard_map/all_to_all | solution.py:647
  12.0 0.0 copy-done.6
  12.0 1.1 phases.1
  13.1 0.0 copy-start.4
  13.1 1.0 copy-done.4
  14.1 3.9 %energies.1.energy_ref = f32[32,32,128]{2,1,0:T(8,128)S(1)} custom-call(s32[8,128]{1,0:T(8,128)S(1)} %get-tuple-element.19.found_ref), custom_call_target="tpu_custom_call" | custom-call | flops 26214400 | bytes 524288 | tf_op jit(solution)/shard_map/energies/pallas_call | solution.py:319
  18.0 0.0 copy-done
  18.0 0.0 copy-start.1
  18.0 1.0 copy-done.1
  19.0 0.0 copy-start.2
  19.0 1.0 copy-done.2
  20.1 0.0 copy-start.3
  20.1 1.0 copy-done.3
  21.1 7.6 %local_slope.1.slope_ref = f32[8,128]{1,0:T(8,128)S(1)} custom-call(f32[32,32,128]{2,1,0:T(8,128)S(1)} %bitcast.19, f32[32,32,128]{2,1,0:T(8,128)S(1)} %bitcast.21, f32[32,32,128]{2,1,0:T(8,128)S(1)} %bitcast.23, f32[32,32,128]{2,1,0:T(8,128)S(1)} %bitcast.25), custom_call_target="tpu_custom_call" | custom-call | flops 402653184 | bytes 2097152 | tf_op jit(solution)/shard_map/local_slope/pallas_call | solution.py:555
  28.7 29.5 %all-to-all-done = f32[32,4,32,128]{3,2,1,0:T(8,128)S(1)} async-done(((f32[32,4,32,128]{3,2,1,0:T(8,128)}), f32[32,4,32,128]{3,2,1,0:T(8,128)S(1)}, u32[]{:S(2)}, u32[]{:S(2)}) %all-to-all-start) | async-done | bytes 2097184 | tf_op jit(solution)/shard_map/all_to_all | solution.py:647
  58.2 3.6 %rotate_rest.1 = f32[4128,128]{1,0:T(8,128)S(1)} custom-call(f32[8,128]{1,0:T(8,128)S(1)} %get-tuple-element.17.tangent_ref, bf16[768,256]{1,0:T(8,128)(2,1)S(1)} %get-tuple-element.18.matrix_ref, f32[8,128]{1,0:T(8,128)S(1)} %local_slope.1.slope_ref, f32[32,32,128]{2,1,0:T(8,128)S(1)} %energies.1.energy_ref, f32[32,128,128]{2,1,0:T(8,128)S(1)} %bitcast.17), custom_call_target="tpu_custom_call" | custom-call | flops 805306368 | bytes 4194304 | tf_op jit(solution)/shard_map/rotate_rest/pallas_call | solution.py:495
  61.8 0.0 copy-start.5
  61.8 55.2 %all_to_all.10 = f32[32,129,1,128]{3,2,1,0:T(1,128)S(1)} all-to-all(f32[32,129,1,128]{3,2,1,0:T(1,128)S(1)} %bitcast.16), channel_id=1, replica_groups=mesh['gx'=2,'gy'=4,'gz'=4] {'gx','gy','gz'}, dimensions={0} | all-to-all | bytes 4227072 | tf_op jit(solution)/shard_map/all_to_all | solution.py:647
  117.0 0.0 copy-done.5
  117.0 2.0 %cost_phase.1 = (f32[32,32,128]{2,1,0:T(8,128)}, f32[32,32,128]{2,1,0:T(8,128)}, f32[32,32,128]{2,1,0:T(8,128)}, f32[32,32,128]{2,1,0:T(8,128)}, f32[1,1]{1,0:T(1,128)}, /*index=5*/f32[1,1]{1,0:T(1,128)}) custom-call(f32[2,32,32,128]{3,2,1,0:T(8,128)S(1)} %bitcast.26, f32[4128,128]{1,0:T(8,128)S(1)} %bitcast.15), custom_call_target="tpu_custom_call" | custom-call | flops 1585152 | bytes 5283840 | tf_op jit(solution)/shard_map/cost_phase/pallas_call | solution.py:629
Async XLA Ops:
  4.0 8.0 %copy-start.6 = (s32[131072]{0:T(1024)S(1)}, s32[131072]{0:T(1024)}, u32[]{:S(2)}) copy-start(s32[131072]{0:T(1024)} %param.11) | copy-start | bytes 1572868
  4.0 13.9 %copy-start = (f32[131072]{0:T(1024)S(1)}, f32[131072]{0:T(1024)}, u32[]{:S(2)}) copy-start(f32[131072]{0:T(1024)} %param.7) | copy-start | bytes 1572868
  4.0 54.1 %all-to-all-start = ((f32[32,4,32,128]{3,2,1,0:T(8,128)}), f32[32,4,32,128]{3,2,1,0:T(8,128)S(1)}, u32[]{:S(2)}, u32[]{:S(2)}) async-start(f32[32,4,32,128]{3,2,1,0:T(8,128)} %rotate_top.1), calls=%async_computation | async-start | bytes 4194304 | tf_op jit(solution)/shard_map/all_to_all | solution.py:647
  13.1 1.0 copy-start.4
  18.0 1.0 copy-start.1
  19.0 1.0 copy-start.2
  20.1 1.0 copy-start.3
  61.8 55.2 %copy-start.5 = (f32[2,1024,128]{2,1,0:T(8,128)S(1)}, f32[2,1024,128]{2,1,0:T(8,128)}, u32[]{:S(2)}) copy-start(f32[2,1024,128]{2,1,0:T(8,128)} %copy-done.4) | copy-start | bytes 3145732

commit v2 on v1

--- a/solution.py
+++ b/solution.py
@@ -52,29 +52,18 @@
     )
 
 
-def rotate_leading(load, store, count, tangent, group_bits=3):
-    finished = 0
-    total = count.bit_length() - 1
-    while finished < total:
-        width = min(group_bits, total - finished)
-        stride = 1 << finished
-        size = 1 << width
-        for base in range(count):
-            if base & (stride * (size - 1)):
-                continue
-            items = [load(base + stride * pos, finished > 0) for pos in range(size)]
-            for bit_pos in range(width):
-                bit = 1 << bit_pos
-                items = [
-                    (
-                        items[pos][0] - tangent * items[pos ^ bit][1],
-                        items[pos][1] + tangent * items[pos ^ bit][0],
-                    )
-                    for pos in range(size)
-                ]
-            for pos in range(size):
-                store(base + stride * pos, items[pos])
-        finished += width
+def rotate_bits(items, tangent):
+    bit = 1
+    while bit < len(items):
+        items = [
+            (
+                items[pos][0] - tangent * items[pos ^ bit][1],
+                items[pos][1] + tangent * items[pos ^ bit][0],
+            )
+            for pos in range(len(items))
+        ]
+        bit *= 2
+    return items
 
 
 def pre_kernel(
@@ -82,51 +71,57 @@
 ):
     count, rows, _ = sr_ref.shape
     tiles = rows // SUB
+    groups = in_sem.shape[0]
+    size = count // groups
     sources = (sr_ref, si_ref, ar_ref, ai_ref)
 
-    def fetch(tile, part):
+    def fetch(group, part):
+        some = pl.ds(group * size, size)
         return pltpu.make_async_copy(
-            sources[part].at[:, pl.ds(tile * SUB, SUB), :],
-            held.at[tile, part],
-            in_sem.at[tile, part],
+            sources[part].at[some], held.at[part, some], in_sem.at[group, part]
         )
 
-    def write(tile, pair):
-        return pltpu.make_async_copy(
-            turned.at[tile, pair],
-            out_ref.at[:, pl.ds(2 * pair, 2), pl.ds(tile * SUB, SUB), :],
-            out_sem.at[tile, pair],
-        )
-
-    for tile in range(tiles):
+    def write(pos):
+        return pltpu.make_async_copy(turned.at[pos], out_ref.at[pos], out_sem.at[pos])
+
+    for group in range(groups):
         for part in range(4):
-            fetch(tile, part).start()
+            fetch(group, part).start()
     sine, cosine = sin_cos(splat(beta_ref))
     tangent = sine / cosine
-    for tile in range(tiles):
-        for pair in range(2):
-            for part in range(2):
-                fetch(tile, 2 * pair + part).wait()
-
-            def load(pos, again):
-                if again:
-                    return turned[tile, pair, pos, 0], turned[tile, pair, pos, 1]
-                return held[tile, 2 * pair, pos], held[tile, 2 * pair + 1, pos]
-
-            def store(pos, item):
-                turned[tile, pair, pos, 0] = item[0]
-                turned[tile, pair, pos, 1] = item[1]
-
-            rotate_leading(load, store, count, tangent)
-            write(tile, pair).start()
-    for tile in range(tiles):
-        for pair in range(2):
-            write(tile, pair).wait()
+
+    def rotated(places, first, here):
+        return rotate_bits(
+            [(held[first, pos, here], held[first + 1, pos, here]) for pos in places], tangent
+        )
+
+    for group in range(groups):
+        places = range(group * size, (group + 1) * size)
+        for first in (0, 2):
+            fetch(group, first).wait()
+            fetch(group, first + 1).wait()
+            for tile in range(tiles):
+                here = pl.ds(tile * SUB, SUB)
+                for pos, item in zip(places, rotated(places, first, here)):
+                    held[first, pos, here] = item[0]
+                    held[first + 1, pos, here] = item[1]
+    for base in range(size):
+        places = range(base, count, size)
+        for first in (0, 2):
+            for tile in range(tiles):
+                here = pl.ds(tile * SUB, SUB)
+                for pos, item in zip(places, rotated(places, first, here)):
+                    turned[pos, first, here] = item[0]
+                    turned[pos, first + 1, here] = item[1]
+        for pos in places:
+            write(pos).start()
+    for pos in range(count):
+        write(pos).wait()
 
 
 def pre_rotate(beta, sr, si, ar, ai):
     count, rows, _ = sr.shape
-    tiles = rows // SUB
+    groups = max(1, count // 8)
     hbm = pl.BlockSpec(memory_space=pltpu.HBM)
     size = count * rows * LANES
     return pl.pallas_call(
@@ -135,10 +130,10 @@
         out_specs=hbm,
         out_shape=jax.ShapeDtypeStruct((count, 4, rows, LANES), jnp.float32),
         scratch_shapes=[
-            pltpu.VMEM((tiles, 4, count, SUB, LANES), jnp.float32),
-            pltpu.VMEM((tiles, 2, count, 2, SUB, LANES), jnp.float32),
-            pltpu.SemaphoreType.DMA((tiles, 4)),
-            pltpu.SemaphoreType.DMA((tiles, 2)),
+            pltpu.VMEM((4, count, rows, LANES), jnp.float32),
+            pltpu.VMEM((count, 4, rows, LANES), jnp.float32),
+            pltpu.SemaphoreType.DMA((groups, 4)),
+            pltpu.SemaphoreType.DMA((count,)),
         ],
         compiler_params=pltpu.CompilerParams(vmem_limit_bytes=LARGE_VMEM_BYTES),
         cost_estimate=pl.CostEstimate(
@@ -348,45 +343,56 @@
     tangent = tangent_ref[...]
     span = max(1, 64 // rows)
 
-    def rows_step(pos, carry):
+    def rotate_rows(pos, pair_pos):
         some = pl.ds(pos * span, span)
         there = pl.ds(pl.multiple_of(pos * (span * rows), span * rows), span * rows)
-        for pair_pos in range(2):
-            pair = [
-                in_ref[some, pl.ds((2 * pair_pos + part) * rows, rows), :].reshape(
-                    span, tiles, SUB, LANES
+        pair = [
+            in_ref[some, pl.ds((2 * pair_pos + part) * rows, rows), :].reshape(
+                span, tiles, SUB, LANES
+            )
+            for part in range(2)
+        ]
+        bit = 1
+        while bit < tiles:
+            other = [
+                jnp.concatenate(
+                    [part[:, tile ^ bit : (tile ^ bit) + 1] for tile in range(tiles)], axis=1
                 )
-                for part in range(2)
+                for part in pair
             ]
-            bit = 1
-            while bit < tiles:
-                other = [
-                    jnp.concatenate(
-                        [part[:, tile ^ bit : (tile ^ bit) + 1] for tile in range(tiles)], axis=1
-                    )
-                    for part in pair
-                ]
-                pair = [pair[0] - tangent * other[1], pair[1] + tangent * other[0]]
-                bit *= 2
-            pair = [part.reshape(span * tiles, SUB, LANES) for part in pair]
-            for bit in (1, 2, 4):
-                other = [flip_sublane(part, bit) for part in pair]
-                pair = [pair[0] - tangent * other[1], pair[1] + tangent * other[0]]
-            for part in range(2):
-                first, second = split_in_two(pair[part].reshape(span * rows, LANES))
-                for place, term in ((0, first), (1, second), (2, first)):
-                    start = (2 * place + part) * LANES
-                    split[pair_pos, there, start : start + LANES] = term
+            pair = [pair[0] - tangent * other[1], pair[1] + tangent * other[0]]
+            bit *= 2
+        pair = [part.reshape(span * tiles, SUB, LANES) for part in pair]
+        for bit in (1, 2, 4):
+            other = [flip_sublane(part, bit) for part in pair]
+            pair = [pair[0] - tangent * other[1], pair[1] + tangent * other[0]]
+        for part in range(2):
+            first, second = split_in_two(pair[part].reshape(span * rows, LANES))
+            for place, term in ((0, first), (1, second), (2, first)):
+                start = (2 * place + part) * LANES
+                split[pair_pos, there, start : start + LANES] = term
+
+    def rotate_lanes(pair_pos, pos):
+        there = pl.ds(pos * half, half)
+        wide[pair_pos, there, :] = jnp.dot(
+            split[pair_pos, there, :], matrix_ref[...], preferred_element_type=jnp.float32
+        )
+
+    half = count * rows // 2
+    steps = count // span
+
+    def two_steps(pos, carry):
+        for more in range(2):
+            rotate_rows(2 * pos + more, 0)
         return carry
 
-    lax.fori_loop(0, count // span, rows_step, 0)
-    half = count * rows // 2
-    for pair_pos in range(2):
-        for pos in range(2):
-            there = pl.ds(pos * half, half)
-            wide[pair_pos, there, :] = jnp.dot(
-                split[pair_pos, there, :], matrix_ref[...], preferred_element_type=jnp.float32
-            )
+    lax.fori_loop(0, steps // 2, two_steps, 0)
+    for pos in range(2):
+        rotate_lanes(0, pos)
+        for step in range(pos * steps // 2, (pos + 1) * steps // 2):
+            rotate_rows(step, 1)
+    for pos in range(2):
+        rotate_lanes(1, pos)
 
     def group(tile, bits, places):
         pairs = []
@@ -395,16 +401,7 @@
             for place in places:
                 here = pl.ds(place * rows + tile * SUB, SUB)
                 items.append([wide[pair_pos, here, :LANES], wide[pair_pos, here, LANES:]])
-            for bit_pos in range(bits):
-                bit = 1 << bit_pos
-                items = [
-                    (
-                        items[pos][0] - tangent * items[pos ^ bit][1],
-                        items[pos][1] + tangent * items[pos ^ bit][0],
-                    )
-                    for pos in range(len(places))
-                ]
-            pairs.append(items)
+            pairs.append(rotate_bits(items, tangent))
         state, adjoint = pairs
         share = 0.0
         for pos in range(len(places)):
@@ -621,7 +618,7 @@
 
 def last_phase(whole_size, phase, returned):
     _, count, rows, _ = phase.shape
-    parts = 4
+    parts = 8
     shape = jax.ShapeDtypeStruct((count, rows, LANES), jnp.float32)
     number = jax.ShapeDtypeStruct((1, 1), jnp.float32)
     vmem = pl.BlockSpec(memory_space=pltpu.VMEM)

time: 119 us -> 120 us (level)
  transfers between devices with their start and end apart: 1 -> 1, of which waited for: 1 -> 1; matrix products, arithmetic and copies ran while one was open for 0% -> 0% of each run, Pallas kernels for 11% -> 10%
where the time goes in v2:
time: 120 us
  blocking collectives  55.2 us (46%)
  waiting for transfers between devices  29.5 us (25%)
  Pallas kernels  21.6 us (18%)
  starting transfers between devices  7.3 us (6%)
  local copies, waits for them, and re-layouts  4.12 us (3%)
  between operations  2.03 us (2%)
    all_to_all x1, blocking collectives, swap(): return lax.all_to_all(values, AXES, split_axis=0, concat_axis=0, tiled=True)  55.2 us
    all_to_all x1, waiting for transfers between devices, swap(): return lax.all_to_all(values, AXES, split_axis=0, concat_axis=0, tiled=True)  29.5 us
    pallas_call x1, Pallas kernels, local_slope(): pl.pallas_call(slope_kernel, in_specs=[vmem] * 4, out_specs=vmem, out_sha...  7.56 us
    all_to_all x1, starting transfers between devices, swap(): return lax.all_to_all(values, AXES, split_axis=0, concat_axis=0, tiled=True)  7.3 us
    unnamed x14, local copies, waits for them, and re-layouts  4.12 us
    pallas_call x1, Pallas kernels, exchanged_energies(): pl.pallas_call(functools.partial(energy_kernel, qubits, table), in_specs=...  3.91 us
    pallas_call x1, Pallas kernels, mid_rotate(): pl.pallas_call(mid_kernel, in_specs=[vmem] * 5, out_specs=vmem, out_shape...  3.52 us
    pallas_call x1, Pallas kernels, pre_rotate(): pl.pallas_call(pre_kernel, in_specs=[pl.BlockSpec(memory_space=pltpu.SMEM...  3.45 us
  transfers between devices with their start and end apart: 1, of which 1 were waited for; matrix products, arithmetic and copies ran while one was open for 0% of the time, Pallas kernels for 10%

profile of v2, /device:TPU:0, one launch (start us, length us, event | category | flops | bytes accessed | tf_op | source)
XLA Modules:
  0.0 119.7 jit_solution(13040539674528327247)
XLA Ops:
  1.3 3.5 %rotate_top.1 = f32[32,4,32,128]{3,2,1,0:T(8,128)} custom-call(f32[1]{0:T(128)S(6)} %copy.15.beta_ref, f32[32,32,128]{2,1,0:T(8,128)} %bitcast.18, f32[32,32,128]{2,1,0:T(8,128)} %bitcast.20, f32[32,32,128]{2,1,0:T(8,128)} %bitcast.22, f32[32,32,128]{2,1,0:T(8,128)} %bitcast.24), custom_call_target="tpu_custom_call" | custom-call | flops 5242880 | bytes 4194304 | tf_op jit(solution)/shard_map/rotate_top/pallas_call | solution.py:127
  4.7 0.0 copy-start.6
  4.7 0.0 copy-start
  4.8 7.3 %all-to-all-start = ((f32[32,4,32,128]{3,2,1,0:T(8,128)}), f32[32,4,32,128]{3,2,1,0:T(8,128)S(1)}, u32[]{:S(2)}, u32[]{:S(2)}) async-start(f32[32,4,32,128]{3,2,1,0:T(8,128)} %rotate_top.1), calls=%async_computation | async-start | bytes 4194304 | tf_op jit(solution)/shard_map/all_to_all | solution.py:644
  12.7 0.0 copy-done.6
  12.7 1.1 phases.1
  13.8 0.0 copy-start.4
  13.8 1.0 copy-done.4
  14.8 3.9 %energies.1.energy_ref = f32[32,32,128]{2,1,0:T(8,128)S(1)} custom-call(s32[8,128]{1,0:T(8,128)S(1)} %get-tuple-element.19.found_ref), custom_call_target="tpu_custom_call" | custom-call | flops 26214400 | bytes 524288 | tf_op jit(solution)/shard_map/energies/pallas_call | solution.py:314
  18.7 0.0 copy-done
  18.7 0.0 copy-start.1
  18.7 1.0 copy-done.1
  19.8 0.0 copy-start.2
  19.8 1.0 copy-done.2
  20.8 0.0 copy-start.3
  20.8 1.0 copy-done.3
  21.8 7.6 %local_slope.1.slope_ref = f32[8,128]{1,0:T(8,128)S(1)} custom-call(f32[32,32,128]{2,1,0:T(8,128)S(1)} %bitcast.19, f32[32,32,128]{2,1,0:T(8,128)S(1)} %bitcast.21, f32[32,32,128]{2,1,0:T(8,128)S(1)} %bitcast.23, f32[32,32,128]{2,1,0:T(8,128)S(1)} %bitcast.25), custom_call_target="tpu_custom_call" | custom-call | flops 402653184 | bytes 2097152 | tf_op jit(solution)/shard_map/local_slope/pallas_call | solution.py:552
  29.4 29.5 %all-to-all-done = f32[32,4,32,128]{3,2,1,0:T(8,128)S(1)} async-done(((f32[32,4,32,128]{3,2,1,0:T(8,128)}), f32[32,4,32,128]{3,2,1,0:T(8,128)S(1)}, u32[]{:S(2)}, u32[]{:S(2)}) %all-to-all-start) | async-done | bytes 2097184 | tf_op jit(solution)/shard_map/all_to_all | solution.py:644
  58.9 3.5 %rotate_rest.1 = f32[4128,128]{1,0:T(8,128)S(1)} custom-call(f32[8,128]{1,0:T(8,128)S(1)} %get-tuple-element.17.tangent_ref, bf16[768,256]{1,0:T(8,128)(2,1)S(1)} %get-tuple-element.18.matrix_ref, f32[8,128]{1,0:T(8,128)S(1)} %local_slope.1.slope_ref, f32[32,32,128]{2,1,0:T(8,128)S(1)} %energies.1.energy_ref, f32[32,128,128]{2,1,0:T(8,128)S(1)} %bitcast.17), custom_call_target="tpu_custom_call" | custom-call | flops 805306368 | bytes 4194304 | tf_op jit(solution)/shard_map/rotate_rest/pallas_call | solution.py:492
  62.4 0.0 copy-start.5
  62.4 55.2 %all_to_all.10 = f32[32,129,1,128]{3,2,1,0:T(1,128)S(1)} all-to-all(f32[32,129,1,128]{3,2,1,0:T(1,128)S(1)} %bitcast.16), channel_id=1, replica_groups=mesh['gx'=2,'gy'=4,'gz'=4] {'gx','gy','gz'}, dimensions={0} | all-to-all | bytes 4227072 | tf_op jit(solution)/shard_map/all_to_all | solution.py:644
  117.6 0.0 copy-done.5
  117.6 2.1 %cost_phase.1 = (f32[32,32,128]{2,1,0:T(8,128)}, f32[32,32,128]{2,1,0:T(8,128)}, f32[32,32,128]{2,1,0:T(8,128)}, f32[32,32,128]{2,1,0:T(8,128)}, f32[1,1]{1,0:T(1,128)}, /*index=5*/f32[1,1]{1,0:T(1,128)}) custom-call(f32[2,32,32,128]{3,2,1,0:T(8,128)S(1)} %bitcast.26, f32[4128,128]{1,0:T(8,128)S(1)} %bitcast.15), custom_call_target="tpu_custom_call" | custom-call | flops 1585152 | bytes 5283840 | tf_op jit(solution)/shard_map/cost_phase/pallas_call | solution.py:626
Async XLA Ops:
  4.7 8.0 %copy-start.6 = (s32[131072]{0:T(1024)S(1)}, s32[131072]{0:T(1024)}, u32[]{:S(2)}) copy-start(s32[131072]{0:T(1024)} %param.11) | copy-start | bytes 1572868
  4.7 13.9 %copy-start = (f32[131072]{0:T(1024)S(1)}, f32[131072]{0:T(1024)}, u32[]{:S(2)}) copy-start(f32[131072]{0:T(1024)} %param.7) | copy-start | bytes 1572868
  4.8 54.1 %all-to-all-start = ((f32[32,4,32,128]{3,2,1,0:T(8,128)}), f32[32,4,32,128]{3,2,1,0:T(8,128)S(1)}, u32[]{:S(2)}, u32[]{:S(2)}) async-start(f32[32,4,32,128]{3,2,1,0:T(8,128)} %rotate_top.1), calls=%async_computation | async-start | bytes 4194304 | tf_op jit(solution)/shard_map/all_to_all | solution.py:644
  13.8 1.0 copy-start.4
  18.7 1.0 copy-start.1
  19.8 1.0 copy-start.2
  20.8 1.0 copy-start.3
  62.4 55.2 %copy-start.5 = (f32[2,1024,128]{2,1,0:T(8,128)S(1)}, f32[2,1024,128]{2,1,0:T(8,128)}, u32[]{:S(2)}) copy-start(f32[2,1024,128]{2,1,0:T(8,128)} %copy-done.4) | copy-start | bytes 3145732

commit v3 on v2

--- a/solution.py
+++ b/solution.py
@@ -9,6 +9,7 @@
 from jax.sharding import PartitionSpec as P
 
 AXES = ("gx", "gy", "gz")
+SWAP_AXES = ("gy", "gx", "gz")
 LANES = 128
 SUB = 8
 VMEM_BYTES = 12 * 1024 * 1024
@@ -66,62 +67,73 @@
     return items
 
 
+def rotate_leading(load, store, count, tangent, group_bits=3):
+    finished = 0
+    total = count.bit_length() - 1
+    while finished < total:
+        width = min(group_bits, total - finished)
+        stride = 1 << finished
+        size = 1 << width
+        for base in range(count):
+            if base & (stride * (size - 1)):
+                continue
+            items = [load(base + stride * pos, finished > 0) for pos in range(size)]
+            items = rotate_bits(items, tangent)
+            for pos in range(size):
+                store(base + stride * pos, items[pos])
+        finished += width
+
+
 def pre_kernel(
     beta_ref, sr_ref, si_ref, ar_ref, ai_ref, out_ref, held, turned, in_sem, out_sem
 ):
     count, rows, _ = sr_ref.shape
     tiles = rows // SUB
-    groups = in_sem.shape[0]
-    size = count // groups
     sources = (sr_ref, si_ref, ar_ref, ai_ref)
 
-    def fetch(group, part):
-        some = pl.ds(group * size, size)
+    def fetch(tile, part):
         return pltpu.make_async_copy(
-            sources[part].at[some], held.at[part, some], in_sem.at[group, part]
+            sources[part].at[:, pl.ds(tile * SUB, SUB), :],
+            held.at[tile, part],
+            in_sem.at[tile, part],
         )
 
-    def write(pos):
-        return pltpu.make_async_copy(turned.at[pos], out_ref.at[pos], out_sem.at[pos])
-
-    for group in range(groups):
+    def write(tile, pair):
+        return pltpu.make_async_copy(
+            turned.at[tile, pair],
+            out_ref.at[:, pl.ds(2 * pair, 2), pl.ds(tile * SUB, SUB), :],
+            out_sem.at[tile, pair],
+        )
+
+    for tile in range(tiles):
         for part in range(4):
-            fetch(group, part).start()
+            fetch(tile, part).start()
     sine, cosine = sin_cos(splat(beta_ref))
     tangent = sine / cosine
-
-    def rotated(places, first, here):
-        return rotate_bits(
-            [(held[first, pos, here], held[first + 1, pos, here]) for pos in places], tangent
-        )
-
-    for group in range(groups):
-        places = range(group * size, (group + 1) * size)
-        for first in (0, 2):
-            fetch(group, first).wait()
-            fetch(group, first + 1).wait()
-            for tile in range(tiles):
-                here = pl.ds(tile * SUB, SUB)
-                for pos, item in zip(places, rotated(places, first, here)):
-                    held[first, pos, here] = item[0]
-                    held[first + 1, pos, here] = item[1]
-    for base in range(size):
-        places = range(base, count, size)
-        for first in (0, 2):
-            for tile in range(tiles):
-                here = pl.ds(tile * SUB, SUB)
-                for pos, item in zip(places, rotated(places, first, here)):
-                    turned[pos, first, here] = item[0]
-                    turned[pos, first + 1, here] = item[1]
-        for pos in places:
-            write(pos).start()
-    for pos in range(count):
-        write(pos).wait()
+    for tile in range(tiles):
+        for pair in range(2):
+            for part in range(2):
+                fetch(tile, 2 * pair + part).wait()
+
+            def load(pos, again):
+                if again:
+                    return turned[tile, pair, pos, 0], turned[tile, pair, pos, 1]
+                return held[tile, 2 * pair, pos], held[tile, 2 * pair + 1, pos]
+
+            def store(pos, item):
+                turned[tile, pair, pos, 0] = item[0]
+                turned[tile, pair, pos, 1] = item[1]
+
+            rotate_leading(load, store, count, tangent)
+            write(tile, pair).start()
+    for tile in range(tiles):
+        for pair in range(2):
+            write(tile, pair).wait()
 
 
 def pre_rotate(beta, sr, si, ar, ai):
     count, rows, _ = sr.shape
-    groups = max(1, count // 8)
+    tiles = rows // SUB
     hbm = pl.BlockSpec(memory_space=pltpu.HBM)
     size = count * rows * LANES
     return pl.pallas_call(
@@ -130,10 +142,10 @@
         out_specs=hbm,
         out_shape=jax.ShapeDtypeStruct((count, 4, rows, LANES), jnp.float32),
         scratch_shapes=[
-            pltpu.VMEM((4, count, rows, LANES), jnp.float32),
-            pltpu.VMEM((count, 4, rows, LANES), jnp.float32),
-            pltpu.SemaphoreType.DMA((groups, 4)),
-            pltpu.SemaphoreType.DMA((count,)),
+            pltpu.VMEM((tiles, 4, count, SUB, LANES), jnp.float32),
+            pltpu.VMEM((tiles, 2, count, 2, SUB, LANES), jnp.float32),
+            pltpu.SemaphoreType.DMA((tiles, 4)),
+            pltpu.SemaphoreType.DMA((tiles, 2)),
         ],
         compiler_params=pltpu.CompilerParams(vmem_limit_bytes=LARGE_VMEM_BYTES),
         cost_estimate=pl.CostEstimate(
@@ -285,10 +297,22 @@
         + lax.broadcasted_iota(jnp.int32, (SUB, LANES), 1)
     ) ^ mask
     tiles = rows // SUB
+    here = lax.axis_index(SWAP_AXES)
+
+    def device_at(pos):
+        places = {}
+        for name in reversed(SWAP_AXES):
+            width = lax.axis_size(name).bit_length() - 1
+            places[name] = pos & ((1 << width) - 1)
+            pos = pos >> width
+        index = 0
+        for name in AXES:
+            index = (index << (lax.axis_size(name).bit_length() - 1)) | places[name]
+        return index
 
     def step(pos, carry):
         for tile in range(tiles):
-            place = (pos << local_bits) + device * block + tile * (SUB * LANES)
+            place = (device_at(pos) << local_bits) + here * block + tile * (SUB * LANES)
             spins = offset ^ place
             energy = jnp.zeros((SUB, LANES), jnp.float32)
             for lag in range(1, qubits):
@@ -576,7 +600,7 @@
             done.at[place, some], out_refs[place].at[some], out_sem.at[pos, place]
         )
 
-    sublane = lax.axis_index(AXES) & (SUB - 1)
+    sublane = lax.axis_index(SWAP_AXES) & (SUB - 1)
     skip = (SUB - sublane) & (SUB - 1)
     below = jnp.where(sublane == SUB - 1, SUB, sublane)
     block_tiles = 4 * tiles
@@ -618,7 +642,7 @@
 
 def last_phase(whole_size, phase, returned):
     _, count, rows, _ = phase.shape
-    parts = 8
+    parts = 4
     shape = jax.ShapeDtypeStruct((count, rows, LANES), jnp.float32)
     number = jax.ShapeDtypeStruct((1, 1), jnp.float32)
     vmem = pl.BlockSpec(memory_space=pltpu.VMEM)
@@ -641,7 +665,7 @@
 
 
 def swap(values):
-    return lax.all_to_all(values, AXES, split_axis=0, concat_axis=0, tiled=True)
+    return lax.all_to_all(values, SWAP_AXES, split_axis=0, concat_axis=0, tiled=True)
 
 
 def per_device(

time: 120 us -> 119 us (level)
  blocking collectives: 55.2 us -> 53.4 us
  waiting for transfers between devices: 29.5 us -> 31.3 us
    all_to_all x1, blocking collectives: 55.2 us -> 53.4 us  [swap(): lax.all_to_all(values, SWAP_AXES, split_axis=0, concat_axis=0, tiled=True)]
    all_to_all x1, waiting for transfers between devices: 29.5 us -> 31.3 us  [swap(): lax.all_to_all(values, SWAP_AXES, split_axis=0, concat_axis=0, tiled=True)]
  transfers between devices with their start and end apart: 1 -> 1, of which waited for: 1 -> 1; matrix products, arithmetic and copies ran while one was open for 0% -> 0% of each run, Pallas kernels for 10% -> 11%
where the time goes in v3:
time: 119 us
  blocking collectives  53.4 us (45%)
  waiting for transfers between devices  31.3 us (26%)
  Pallas kernels  20.9 us (18%)
  starting transfers between devices  7.3 us (6%)
  local copies, waits for them, and re-layouts  4.12 us (3%)
  between operations  2.03 us (2%)
    all_to_all x1, blocking collectives, swap(): lax.all_to_all(values, SWAP_AXES, split_axis=0, concat_axis=0, tiled=True)  53.4 us
    all_to_all x1, waiting for transfers between devices, swap(): lax.all_to_all(values, SWAP_AXES, split_axis=0, concat_axis=0, tiled=True)  31.3 us
    pallas_call x1, Pallas kernels, local_slope(): pl.pallas_call(slope_kernel, in_specs=[vmem] * 4, out_specs=vmem, out_sha...  7.56 us
    all_to_all x1, starting transfers between devices, swap(): lax.all_to_all(values, SWAP_AXES, split_axis=0, concat_axis=0, tiled=True)  7.3 us
    unnamed x14, local copies, waits for them, and re-layouts  4.12 us
    pallas_call x1, Pallas kernels, exchanged_energies(): pl.pallas_call(functools.partial(energy_kernel, qubits, table), in_specs=...  4.01 us
    pallas_call x1, Pallas kernels, mid_rotate(): pl.pallas_call(mid_kernel, in_specs=[vmem] * 5, out_specs=vmem, out_shape...  3.52 us
    pallas_call x1, Pallas kernels, pre_rotate(): pl.pallas_call(pre_kernel, in_specs=[pl.BlockSpec(memory_space=pltpu.SMEM...  2.73 us
  transfers between devices with their start and end apart: 1, of which 1 were waited for; matrix products, arithmetic and copies ran while one was open for 0% of the time, Pallas kernels for 11%

profile of v3, /device:TPU:0, one launch (start us, length us, event | category | flops | bytes accessed | tf_op | source)
XLA Modules:
  0.0 119.0 jit_solution(9337594976952979098)
XLA Ops:
  1.3 2.7 %rotate_top.1 = f32[32,4,32,128]{3,2,1,0:T(8,128)} custom-call(f32[1]{0:T(128)S(6)} %copy.15.beta_ref, f32[32,32,128]{2,1,0:T(8,128)} %bitcast.18, f32[32,32,128]{2,1,0:T(8,128)} %bitcast.20, f32[32,32,128]{2,1,0:T(8,128)} %bitcast.22, f32[32,32,128]{2,1,0:T(8,128)} %bitcast.24), custom_call_target="tpu_custom_call" | custom-call | flops 5242880 | bytes 4194304 | tf_op jit(solution)/shard_map/rotate_top/pallas_call | solution.py:139
  4.0 0.0 copy-start.6
  4.0 0.0 copy-start
  4.0 7.3 %all-to-all-start = ((f32[32,4,32,128]{3,2,1,0:T(8,128)}), f32[32,4,32,128]{3,2,1,0:T(8,128)S(1)}, u32[]{:S(2)}, u32[]{:S(2)}) async-start(f32[32,4,32,128]{3,2,1,0:T(8,128)} %rotate_top.1), calls=%async_computation | async-start | bytes 4194304 | tf_op jit(solution)/shard_map/all_to_all | solution.py:668
  12.0 0.0 copy-done.6
  12.0 1.1 phases.1
  13.1 0.0 copy-start.4
  13.1 1.0 copy-done.4
  14.1 4.0 %energies.1.energy_ref = f32[32,32,128]{2,1,0:T(8,128)S(1)} custom-call(s32[8,128]{1,0:T(8,128)S(1)} %get-tuple-element.19.found_ref), custom_call_target="tpu_custom_call" | custom-call | flops 26214400 | bytes 524288 | tf_op jit(solution)/shard_map/energies/pallas_call | solution.py:338
  18.1 0.0 copy-done
  18.1 0.0 copy-start.1
  18.1 1.0 copy-done.1
  19.1 0.0 copy-start.2
  19.1 1.0 copy-done.2
  20.2 0.0 copy-start.3
  20.2 1.0 copy-done.3
  21.2 7.6 %local_slope.1.slope_ref = f32[8,128]{1,0:T(8,128)S(1)} custom-call(f32[32,32,128]{2,1,0:T(8,128)S(1)} %bitcast.19, f32[32,32,128]{2,1,0:T(8,128)S(1)} %bitcast.21, f32[32,32,128]{2,1,0:T(8,128)S(1)} %bitcast.23, f32[32,32,128]{2,1,0:T(8,128)S(1)} %bitcast.25), custom_call_target="tpu_custom_call" | custom-call | flops 402653184 | bytes 2097152 | tf_op jit(solution)/shard_map/local_slope/pallas_call | solution.py:576
  28.8 31.3 %all-to-all-done = f32[32,4,32,128]{3,2,1,0:T(8,128)S(1)} async-done(((f32[32,4,32,128]{3,2,1,0:T(8,128)}), f32[32,4,32,128]{3,2,1,0:T(8,128)S(1)}, u32[]{:S(2)}, u32[]{:S(2)}) %all-to-all-start) | async-done | bytes 2097184 | tf_op jit(solution)/shard_map/all_to_all | solution.py:668
  60.0 3.5 %rotate_rest.1 = f32[4128,128]{1,0:T(8,128)S(1)} custom-call(f32[8,128]{1,0:T(8,128)S(1)} %get-tuple-element.17.tangent_ref, bf16[768,256]{1,0:T(8,128)(2,1)S(1)} %get-tuple-element.18.matrix_ref, f32[8,128]{1,0:T(8,128)S(1)} %local_slope.1.slope_ref, f32[32,32,128]{2,1,0:T(8,128)S(1)} %energies.1.energy_ref, f32[32,128,128]{2,1,0:T(8,128)S(1)} %bitcast.17), custom_call_target="tpu_custom_call" | custom-call | flops 805306368 | bytes 4194304 | tf_op jit(solution)/shard_map/rotate_rest/pallas_call | solution.py:516
  63.6 0.0 copy-start.5
  63.6 53.4 %all_to_all.10 = f32[32,129,1,128]{3,2,1,0:T(1,128)S(1)} all-to-all(f32[32,129,1,128]{3,2,1,0:T(1,128)S(1)} %bitcast.16), channel_id=1, replica_groups=mesh['gx'=2,'gy'=4,'gz'=4] {'gy','gx','gz'}, dimensions={0} | all-to-all | bytes 4227072 | tf_op jit(solution)/shard_map/all_to_all | solution.py:668
  117.0 0.0 copy-done.5
  117.0 2.0 %cost_phase.1 = (f32[32,32,128]{2,1,0:T(8,128)}, f32[32,32,128]{2,1,0:T(8,128)}, f32[32,32,128]{2,1,0:T(8,128)}, f32[32,32,128]{2,1,0:T(8,128)}, f32[1,1]{1,0:T(1,128)}, /*index=5*/f32[1,1]{1,0:T(1,128)}) custom-call(f32[2,32,32,128]{3,2,1,0:T(8,128)S(1)} %bitcast.26, f32[4128,128]{1,0:T(8,128)S(1)} %bitcast.15), custom_call_target="tpu_custom_call" | custom-call | flops 1585152 | bytes 5283840 | tf_op jit(solution)/shard_map/cost_phase/pallas_call | solution.py:650
Async XLA Ops:
  4.0 8.0 %copy-start.6 = (s32[131072]{0:T(1024)S(1)}, s32[131072]{0:T(1024)}, u32[]{:S(2)}) copy-start(s32[131072]{0:T(1024)} %param.11) | copy-start | bytes 1572868
  4.0 14.0 %copy-start = (f32[131072]{0:T(1024)S(1)}, f32[131072]{0:T(1024)}, u32[]{:S(2)}) copy-start(f32[131072]{0:T(1024)} %param.7) | copy-start | bytes 1572868
  4.0 56.0 %all-to-all-start = ((f32[32,4,32,128]{3,2,1,0:T(8,128)}), f32[32,4,32,128]{3,2,1,0:T(8,128)S(1)}, u32[]{:S(2)}, u32[]{:S(2)}) async-start(f32[32,4,32,128]{3,2,1,0:T(8,128)} %rotate_top.1), calls=%async_computation | async-start | bytes 4194304 | tf_op jit(solution)/shard_map/all_to_all | solution.py:668
  13.1 1.0 copy-start.4
  18.1 1.0 copy-start.1
  19.1 1.0 copy-start.2
  20.2 1.0 copy-start.3
  63.6 53.4 %copy-start.5 = (f32[2,1024,128]{2,1,0:T(8,128)S(1)}, f32[2,1024,128]{2,1,0:T(8,128)}, u32[]{:S(2)}) copy-start(f32[2,1024,128]{2,1,0:T(8,128)} %copy-done.4) | copy-start | bytes 3145732

commit v4 on v3

--- a/solution.py
+++ b/solution.py
@@ -9,7 +9,6 @@
 from jax.sharding import PartitionSpec as P
 
 AXES = ("gx", "gy", "gz")
-SWAP_AXES = ("gy", "gx", "gz")
 LANES = 128
 SUB = 8
 VMEM_BYTES = 12 * 1024 * 1024
@@ -156,7 +155,7 @@
 
 
 def prep_kernel(
-    qubits, beta_ref, gamma_ref, energy_ref, matrix_ref, tangent_ref, phase_ref, found_ref
+    qubits, beta_ref, energy_ref, matrix_ref, tangent_ref, found_ref
 ):
     sine, cosine = sin_cos(splat(beta_ref))
     tangent_ref[...] = sine / cosine
@@ -198,7 +197,6 @@
 
     local_size = energy_ref.shape[0] * LANES
     tiles = 4 * SUB
-    gamma = gamma_ref[0]
 
     def step(pos, best):
         rows = pl.ds(pl.multiple_of(pos * tiles, tiles), tiles)
@@ -208,9 +206,6 @@
             + lax.broadcasted_iota(jnp.int32, energy.shape, 1)
             + pos * (tiles * LANES)
         )
-        sine_part, cosine_part = sin_cos(gamma * energy.astype(jnp.float32))
-        phase_ref[0, rows, :] = cosine_part
-        phase_ref[1, rows, :] = sine_part
         return jnp.maximum(best, energy * local_size + index)
 
     best = lax.fori_loop(
@@ -219,26 +214,56 @@
     found_ref[...] = jnp.max(best.reshape(-1, SUB, LANES), axis=0)
 
 
-def prepare(qubits, beta, gamma, energies):
+def prepare(qubits, beta, energies):
     rows = energies.shape[0]
     smem = pl.BlockSpec(memory_space=pltpu.SMEM)
     vmem = pl.BlockSpec(memory_space=pltpu.VMEM)
     return pl.pallas_call(
         functools.partial(prep_kernel, qubits),
-        in_specs=[smem, smem, vmem],
-        out_specs=[vmem] * 4,
+        in_specs=[smem, vmem],
+        out_specs=[vmem] * 3,
         out_shape=[
             jax.ShapeDtypeStruct((6 * LANES, 2 * LANES), jnp.bfloat16),
             jax.ShapeDtypeStruct((SUB, LANES), jnp.float32),
-            jax.ShapeDtypeStruct((2, rows, LANES), jnp.float32),
             jax.ShapeDtypeStruct((SUB, LANES), jnp.int32),
         ],
+        compiler_params=pltpu.CompilerParams(vmem_limit_bytes=VMEM_BYTES),
+        cost_estimate=pl.CostEstimate(
+            flops=rows * LANES * 4, bytes_accessed=rows * LANES * 4, transcendentals=0
+        ),
+        name="lane_matrix",
+    )(beta, energies)
+
+
+def phase_kernel(token_ref, gamma_ref, energy_ref, phase_ref):
+    gamma = gamma_ref[0]
+    tiles = 4 * SUB
+
+    def step(pos, carry):
+        rows = pl.ds(pl.multiple_of(pos * tiles, tiles), tiles)
+        sine, cosine = sin_cos(gamma * energy_ref[rows, :].astype(jnp.float32))
+        phase_ref[0, rows, :] = cosine
+        phase_ref[1, rows, :] = sine
+        return carry
+
+    lax.fori_loop(0, energy_ref.shape[0] // tiles, step, 0)
+
+
+def cost_phases(token, gamma, energies):
+    rows = energies.shape[0]
+    smem = pl.BlockSpec(memory_space=pltpu.SMEM)
+    vmem = pl.BlockSpec(memory_space=pltpu.VMEM)
+    return pl.pallas_call(
+        phase_kernel,
+        in_specs=[vmem, smem, vmem],
+        out_specs=vmem,
+        out_shape=jax.ShapeDtypeStruct((2, rows, LANES), jnp.float32),
         compiler_params=pltpu.CompilerParams(vmem_limit_bytes=VMEM_BYTES),
         cost_estimate=pl.CostEstimate(
             flops=rows * LANES * 50, bytes_accessed=rows * LANES * 12, transcendentals=0
         ),
         name="phases",
-    )(beta, gamma, energies)
+    )(token, gamma, energies)
 
 
 def labs_energy(spins, qubits, count_ones):
@@ -275,7 +300,7 @@
     return table
 
 
-def energy_kernel(qubits, table, found_ref, out_ref):
+def energy_kernel(qubits, table, found_ref, token_ref, out_ref):
     count, rows, _ = out_ref.shape
     block = rows * LANES
     local_bits = (count * block).bit_length() - 1
@@ -297,22 +322,10 @@
         + lax.broadcasted_iota(jnp.int32, (SUB, LANES), 1)
     ) ^ mask
     tiles = rows // SUB
-    here = lax.axis_index(SWAP_AXES)
-
-    def device_at(pos):
-        places = {}
-        for name in reversed(SWAP_AXES):
-            width = lax.axis_size(name).bit_length() - 1
-            places[name] = pos & ((1 << width) - 1)
-            pos = pos >> width
-        index = 0
-        for name in AXES:
-            index = (index << (lax.axis_size(name).bit_length() - 1)) | places[name]
-        return index
 
     def step(pos, carry):
         for tile in range(tiles):
-            place = (device_at(pos) << local_bits) + here * block + tile * (SUB * LANES)
+            place = (pos << local_bits) + device * block + tile * (SUB * LANES)
             spins = offset ^ place
             energy = jnp.zeros((SUB, LANES), jnp.float32)
             for lag in range(1, qubits):
@@ -326,7 +339,7 @@
     lax.fori_loop(0, count, step, 0)
 
 
-def exchanged_energies(qubits, shape, found):
+def exchanged_energies(qubits, shape, found, token):
     local_bits = (shape[0] * shape[1] * shape[2]).bit_length() - 1
     table = highest_table(qubits, local_bits)
     if table is None:
@@ -337,7 +350,7 @@
     vmem = pl.BlockSpec(memory_space=pltpu.VMEM)
     return pl.pallas_call(
         functools.partial(energy_kernel, qubits, table),
-        in_specs=[vmem],
+        in_specs=[vmem, vmem],
         out_specs=vmem,
         out_shape=jax.ShapeDtypeStruct(shape, jnp.float32),
         compiler_params=pltpu.CompilerParams(vmem_limit_bytes=VMEM_BYTES),
@@ -345,7 +358,7 @@
             flops=(200 << local_bits), bytes_accessed=(4 << local_bits), transcendentals=0
         ),
         name="energies",
-    )(found)
+    )(found, token)
 
 
 def tile_place(place, number, tiles):
@@ -360,11 +373,25 @@
 
 
 def mid_kernel(
-    tangent_ref, matrix_ref, slope_ref, energy_ref, in_ref, out_ref, split, wide, edge
+    tangent_ref,
+    matrix_ref,
+    slope_ref,
+    energy_ref,
+    in_ref,
+    out_ref,
+    token_ref,
+    energies,
+    split,
+    wide,
+    edge,
+    energy_sem,
 ):
     count, rows, _ = energy_ref.shape
     tiles = rows // SUB
+    fetch = pltpu.make_async_copy(energy_ref, energies, energy_sem)
+    fetch.start()
     tangent = tangent_ref[...]
+    token_ref[...] = tangent
     span = max(1, 64 // rows)
 
     def rotate_rows(pos, pair_pos):
@@ -417,6 +444,7 @@
             rotate_rows(step, 1)
     for pos in range(2):
         rotate_lanes(1, pos)
+    fetch.wait()
 
     def group(tile, bits, places):
         pairs = []
@@ -474,7 +502,7 @@
             beta_sum = beta_sum + share
             for pos, place in enumerate(places):
                 value = adjoint[pos][0] * state[pos][1] - adjoint[pos][1] * state[pos][0]
-                energy = energy_ref[place, pl.ds(tile * SUB, SUB), :]
+                energy = energies[place, pl.ds(tile * SUB, SUB), :]
                 gamma_sum = gamma_sum + energy * value
                 for part in range(4):
                     item = pairs[part // 2][pos][part % 2]
@@ -515,13 +543,18 @@
     vmem = pl.BlockSpec(memory_space=pltpu.VMEM)
     return pl.pallas_call(
         mid_kernel,
-        in_specs=[vmem] * 5,
-        out_specs=vmem,
-        out_shape=jax.ShapeDtypeStruct(out_shape, jnp.float32),
+        in_specs=[vmem, vmem, vmem, pl.BlockSpec(memory_space=pltpu.HBM), vmem],
+        out_specs=[vmem, vmem],
+        out_shape=[
+            jax.ShapeDtypeStruct(out_shape, jnp.float32),
+            jax.ShapeDtypeStruct((SUB, LANES), jnp.float32),
+        ],
         scratch_shapes=[
+            pltpu.VMEM(energies.shape, jnp.float32),
             pltpu.VMEM(flat + (6 * LANES,), jnp.bfloat16),
             pltpu.VMEM(flat + (2 * LANES,), jnp.float32),
             pltpu.VMEM((count, SUB, LANES), jnp.float32),
+            pltpu.SemaphoreType.DMA,
         ],
         compiler_params=pltpu.CompilerParams(vmem_limit_bytes=MID_VMEM_BYTES),
         cost_estimate=pl.CostEstimate(
@@ -590,17 +623,17 @@
     out_refs, (gamma_ref, beta_ref, done, out_sem) = refs[:4], refs[4:]
     _, count, rows, _ = phase_ref.shape
     parts = out_sem.shape[0]
-    share = count // parts
+    bounds = [count * place // 16 for place in (0, 2, 7, 13, 16)]
     tiles = rows // SUB
     row = lax.broadcasted_iota(jnp.int32, (SUB, LANES), 0)
 
     def write(pos, place):
-        some = pl.ds(pos * share, share)
+        some = pl.ds(bounds[pos], bounds[pos + 1] - bounds[pos])
         return pltpu.make_async_copy(
             done.at[place, some], out_refs[place].at[some], out_sem.at[pos, place]
         )
 
-    sublane = lax.axis_index(SWAP_AXES) & (SUB - 1)
+    sublane = lax.axis_index(AXES) & (SUB - 1)
     skip = (SUB - sublane) & (SUB - 1)
     below = jnp.where(sublane == SUB - 1, SUB, sublane)
     block_tiles = 4 * tiles
@@ -617,7 +650,7 @@
         return jnp.where(sublane == 0, whole, jnp.where(row < below, last, first))
 
     for part in range(parts):
-        for pos in range(part * share, (part + 1) * share):
+        for pos in range(bounds[part], bounds[part + 1]):
             for tile in range(tiles):
                 here = pl.ds(tile * SUB, SUB)
                 cosine, sine = phase_ref[0, pos, here], phase_ref[1, pos, here]
@@ -665,7 +698,7 @@
 
 
 def swap(values):
-    return lax.all_to_all(values, SWAP_AXES, split_axis=0, concat_axis=0, tiled=True)
+    return lax.all_to_all(values, AXES, split_axis=0, concat_axis=0, tiled=True)
 
 
 def per_device(
@@ -680,13 +713,13 @@
         part.reshape(shape) for part in (state_real, state_imag, adjoint_real, adjoint_imag)
     ]
     there = swap(pre_rotate(beta_angle, *arrays)).reshape(devices, -1, LANES)
-    matrix, tangent, phase, found = prepare(
-        qubits, beta_angle, gamma_angle, energies.reshape(-1, LANES)
-    )
-    elsewhere = exchanged_energies(qubits, shape, found)
+    energies = energies.reshape(-1, LANES)
+    matrix, tangent, found = prepare(qubits, beta_angle, energies)
     slope = local_slope(*arrays)
-    middle = mid_rotate(tangent, matrix, slope, elsewhere, there)
+    elsewhere = exchanged_energies(qubits, shape, found, slope)
+    middle, token = mid_rotate(tangent, matrix, slope, elsewhere, there)
     back = swap(middle.reshape(devices, -1, 1, LANES)).reshape(middle.shape)
+    phase = cost_phases(token, gamma_angle, energies)
     *outputs, gamma_gradient, beta_gradient = last_phase(
         whole_size, phase.reshape((2,) + shape), back
     )

time: 119 us -> 119 us (level); the launches traced: 119 us -> 117 us
  blocking collectives: 53.4 us -> 0 us
  waiting for transfers between devices: 31.3 us -> 76.4 us
  starting transfers between devices: 7.3 us -> 11.9 us
  local copies, waits for them, and re-layouts: 4.12 us -> 5.5 us
    all_to_all x1 -> x0, blocking collectives: 53.4 us -> none  [swap(): lax.all_to_all(values, SWAP_AXES, split_axis=0, concat_axis=0, tiled=True)]
    all_to_all x1 -> x2, waiting for transfers between devices: 31.3 us -> 76.4 us  [swap(): return lax.all_to_all(values, AXES, split_axis=0, concat_axis=0, tiled=True)]
    all_to_all x1 -> x2, starting transfers between devices: 7.3 us -> 11.9 us  [swap(): return lax.all_to_all(values, AXES, split_axis=0, concat_axis=0, tiled=True)]
    unnamed x14, local copies, waits for them, and re-layouts: 4.12 us -> 5.5 us
    pallas_call x2 -> x3, Pallas kernels: 4.57 us -> 4.77 us  [the longest x1 3.59 us: mid_rotate(): pl.pallas_call(mid_kernel, in_specs=[vmem, vmem, vmem, pl.BlockSpec(memor...]
  transfers between devices with their start and end apart: 1 -> 2, of which waited for: 1 -> 2; matrix products, arithmetic and copies ran while one was open for 0% -> 0% of each run, Pallas kernels for 11% -> 11%
where the time goes in v4:
time: 119 us; the launch traced here: 117 us
  waiting for transfers between devices  76.4 us (64%)
  Pallas kernels  21.1 us (18%)
  starting transfers between devices  11.9 us (10%)
  local copies, waits for them, and re-layouts  5.5 us (5%)
  between operations  2.05 us (2%)
    all_to_all x2, waiting for transfers between devices, swap(): return lax.all_to_all(values, AXES, split_axis=0, concat_axis=0, tiled=True)  76.4 us
    all_to_all x2, starting transfers between devices, swap(): return lax.all_to_all(values, AXES, split_axis=0, concat_axis=0, tiled=True)  11.9 us
    pallas_call x1, Pallas kernels, local_slope(): pl.pallas_call(slope_kernel, in_specs=[vmem] * 4, out_specs=vmem, out_sha...  7.61 us
    unnamed x14, local copies, waits for them, and re-layouts  5.5 us
    pallas_call x1, Pallas kernels, exchanged_energies(): pl.pallas_call(functools.partial(energy_kernel, qubits, table), in_specs=...  3.92 us
    pallas_call x1, Pallas kernels, mid_rotate(): pl.pallas_call(mid_kernel, in_specs=[vmem, vmem, vmem, pl.BlockSpec(memor...  3.59 us
    pallas_call x1, Pallas kernels, pre_rotate(): pl.pallas_call(pre_kernel, in_specs=[pl.BlockSpec(memory_space=pltpu.SMEM...  2.75 us
  transfers between devices with their start and end apart: 2, of which 2 were waited for; matrix products, arithmetic and copies ran while one was open for 0% of the time, Pallas kernels for 11%

profile of v4, /device:TPU:0, one launch (start us, length us, event | category | flops | bytes accessed | tf_op | source)
XLA Modules:
  0.0 116.9 jit_solution(11767027311348956642)
XLA Ops:
  1.3 2.8 %rotate_top.1 = f32[32,4,32,128]{3,2,1,0:T(8,128)} custom-call(f32[1]{0:T(128)S(6)} %copy.15.beta_ref, f32[32,32,128]{2,1,0:T(8,128)} %bitcast.19, f32[32,32,128]{2,1,0:T(8,128)} %bitcast.21, f32[32,32,128]{2,1,0:T(8,128)} %bitcast.23, f32[32,32,128]{2,1,0:T(8,128)} %bitcast.25), custom_call_target="tpu_custom_call" | custom-call | flops 5242880 | bytes 4194304 | tf_op jit(solution)/shard_map/rotate_top/pallas_call | solution.py:138
  4.0 0.0 copy-start.1
  4.1 0.0 copy-start.2
  4.1 7.3 %all-to-all-start = ((f32[32,4,32,128]{3,2,1,0:T(8,128)}), f32[32,4,32,128]{3,2,1,0:T(8,128)S(1)}, u32[]{:S(2)}, u32[]{:S(2)}) async-start(f32[32,4,32,128]{3,2,1,0:T(8,128)} %rotate_top.1), calls=%async_computation | async-start | bytes 4194304 | tf_op jit(solution)/shard_map/all_to_all | solution.py:701
  11.4 0.0 copy-start.5
  11.4 1.0 copy-done.5
  12.4 0.3 lane_matrix.1
  12.8 0.0 copy-done.1
  12.8 0.0 copy-done.2
  12.8 0.0 copy-start.3
  12.8 1.0 copy-done.3
  13.8 1.0 copy-done.4
  14.9 7.6 %local_slope.1.token_ref.slope_ref = f32[8,128]{1,0:T(8,128)S(1)} custom-call(f32[32,32,128]{2,1,0:T(8,128)S(1)} %bitcast.20, f32[32,32,128]{2,1,0:T(8,128)S(1)} %bitcast.22, f32[32,32,128]{2,1,0:T(8,128)S(1)} %bitcast.24, f32[32,32,128]{2,1,0:T(8,128)S(1)} %bitcast.26), custom_call_target="tpu_custom_call" | custom-call | flops 402653184 | bytes 2097152 | tf_op jit(solution)/shard_map/local_slope/pallas_call | solution.py:609
  22.5 3.9 %energies.1.energy_ref = f32[32,32,128]{2,1,0:T(8,128)S(1)} custom-call(s32[8,128]{1,0:T(8,128)S(1)} %get-tuple-element.19.found_ref, f32[8,128]{1,0:T(8,128)S(1)} %local_slope.1.token_ref.slope_ref), custom_call_target="tpu_custom_call" | custom-call | flops 26214400 | bytes 524288 | tf_op jit(solution)/shard_map/energies/pallas_call | solution.py:351
  26.4 31.8 %all-to-all-done = f32[32,4,32,128]{3,2,1,0:T(8,128)S(1)} async-done(((f32[32,4,32,128]{3,2,1,0:T(8,128)}), f32[32,4,32,128]{3,2,1,0:T(8,128)S(1)}, u32[]{:S(2)}, u32[]{:S(2)}) %all-to-all-start) | async-done | bytes 2097184 | tf_op jit(solution)/shard_map/all_to_all | solution.py:701
  58.2 3.6 %rotate_rest.1 = (f32[4128,128]{1,0:T(8,128)S(1)}, f32[8,128]{1,0:T(8,128)S(1)}) custom-call(f32[8,128]{1,0:T(8,128)S(1)} %get-tuple-element.17.tangent_ref, bf16[768,256]{1,0:T(8,128)(2,1)S(1)} %get-tuple-element.18.matrix_ref, f32[8,128]{1,0:T(8,128)S(1)} %local_slope.1.token_ref.slope_ref, f32[32,32,128]{2,1,0:T(8,128)S(1)} %energies.1.energy_ref, ...), custom_call_target="tpu_custom_call" | custom-call | flops 805306368 | bytes 4194304 | tf_op jit(solution)/shard_map/rotate_rest/pallas_call | solution.py:544
  61.8 0.0 copy-start
  61.8 1.3 %copy-done = f32[4128,128]{1,0:T(8,128)} copy-done((f32[4128,128]{1,0:T(8,128)}, f32[4128,128]{1,0:T(8,128)S(1)}, u32[]{:S(2)}) %copy-start) | copy-done | bytes 2113560
  63.1 4.6 %all-to-all-start.1 = ((f32[32,129,1,128]{3,2,1,0:T(1,128)}), f32[32,129,1,128]{3,2,1,0:T(1,128)S(1)}, u32[]{:S(2)}, u32[]{:S(2)}) async-start(f32[32,129,1,128]{3,2,1,0:T(1,128)} %bitcast.18), calls=%async_computation.1 | async-start | bytes 4227072 | tf_op jit(solution)/shard_map/all_to_all | solution.py:701
  68.4 0.0 copy-start.6
  68.4 1.0 copy-done.6
  69.4 0.9 phases.1
  70.3 44.6 %all-to-all-done.1 = f32[32,129,1,128]{3,2,1,0:T(1,128)S(1)} async-done(((f32[32,129,1,128]{3,2,1,0:T(1,128)}), f32[32,129,1,128]{3,2,1,0:T(1,128)S(1)}, u32[]{:S(2)}, u32[]{:S(2)}) %all-to-all-start.1) | async-done | bytes 2113568 | tf_op jit(solution)/shard_map/all_to_all | solution.py:701
  114.9 2.0 %cost_phase.1 = (f32[32,32,128]{2,1,0:T(8,128)}, f32[32,32,128]{2,1,0:T(8,128)}, f32[32,32,128]{2,1,0:T(8,128)}, f32[32,32,128]{2,1,0:T(8,128)}, f32[1,1]{1,0:T(1,128)}, /*index=5*/f32[1,1]{1,0:T(1,128)}) custom-call(f32[2,32,32,128]{3,2,1,0:T(8,128)S(1)} %bitcast.17, f32[4128,128]{1,0:T(8,128)S(1)} %bitcast.15), custom_call_target="tpu_custom_call" | custom-call | flops 1585152 | bytes 5283840 | tf_op jit(solution)/shard_map/cost_phase/pallas_call | solution.py:683
  (1 shorter events, 0.0 us)
Async XLA Ops:
  4.0 8.7 %copy-start.1 = (f32[131072]{0:T(1024)S(1)}, f32[131072]{0:T(1024)}, u32[]{:S(2)}) copy-start(f32[131072]{0:T(1024)} %param.7) | copy-start | bytes 1572868
  4.1 8.7 %copy-start.2 = (f32[131072]{0:T(1024)S(1)}, f32[131072]{0:T(1024)}, u32[]{:S(2)}) copy-start(f32[131072]{0:T(1024)} %param.8) | copy-start | bytes 1572868
  4.1 54.1 %all-to-all-start = ((f32[32,4,32,128]{3,2,1,0:T(8,128)}), f32[32,4,32,128]{3,2,1,0:T(8,128)S(1)}, u32[]{:S(2)}, u32[]{:S(2)}) async-start(f32[32,4,32,128]{3,2,1,0:T(8,128)} %rotate_top.1), calls=%async_computation | async-start | bytes 4194304 | tf_op jit(solution)/shard_map/all_to_all | solution.py:701
  11.4 1.0 copy-start.5
  12.8 1.0 copy-start.3
  13.8 1.0 copy-start.4
  61.8 1.3 %copy-start = (f32[4128,128]{1,0:T(8,128)}, f32[4128,128]{1,0:T(8,128)S(1)}, u32[]{:S(2)}) copy-start(f32[4128,128]{1,0:T(8,128)S(1)} %get-tuple-element.21) | copy-start | bytes 6340612
  63.1 51.8 %all-to-all-start.1 = ((f32[32,129,1,128]{3,2,1,0:T(1,128)}), f32[32,129,1,128]{3,2,1,0:T(1,128)S(1)}, u32[]{:S(2)}, u32[]{:S(2)}) async-start(f32[32,129,1,128]{3,2,1,0:T(1,128)} %bitcast.18), calls=%async_computation.1 | async-start | bytes 4227072 | tf_op jit(solution)/shard_map/all_to_all | solution.py:701
  68.4 1.0 copy-start.6
